TPU v7x, 256 devices: a whole 4x4x8 slice. The times are simulated.
256 devices in a mesh: section: 16 (over y, z_hi), tensor: 16 (over x, z_lo, core).
Axes of the slice: x: 4, y: 4, z: 8 (z_hi: 4, z_lo: 2; z = z_hi * 2 + z_lo), core: 2. Of those that a mesh axis runs over, the one named last changes fastest.
Arguments:
- store: bfloat16 [64, 640, 2048], P('section', None, 'tensor'), as said below
- owners: int32 [16], replicated, may hold values from 0 to 63, as said below
- positions: int32 [16], replicated, may hold values from 0 to 9600, as said below
- sel_rows: int32 [16, 96], replicated, may hold values from 0 to 639, as said below
- sel_hidden: bfloat16 [16, 96, 12288], P(None, None, 'section'), as said below
- norm_gain: bfloat16 [12288], P('section'), may hold values from 0.099609375 to 1.8984375
- w_query: bfloat16 [12288, 12288], P('section', 'tensor'), may hold values from -0.0546875 to 0.0546875
- w_keyval: bfloat16 [12288, 2048], P('section', 'tensor'), may hold values from -0.0546875 to 0.0546875
- w_out: bfloat16 [12288, 12288], P('tensor', 'section'), may hold values from -0.5 to 0.5
Outputs:
- blended_cache: bfloat16 [16, 640, 2048], P('section', None, 'tensor')
- mixed: bfloat16 [16, 96, 12288], P('tensor', None, 'section')
Inputs may be any that keep to these rules, and one draw needn't show every extreme that they name: `owners`: slot of each group's cache; slot s lies on section index s // 4. Groups use distinct slots, and one section index holds 4 of the groups in every draw. `positions`: 640 times a permutation of the group numbers. `sel_rows`: 96 distinct rows of each group, in increasing order. `store`: cached keys and values of each slot. `sel_hidden`: hidden states at the recomputed rows.
All inputs are finite; a program needn't handle non-finite values.
Results may differ from a plain program's by a relative error of at most 0.025.
The roundings to bfloat16 on the way count: a program that leaves them out, or rounds other values in their place, can miss the bound.
Values may be sent and summed in bfloat16 or wider, within the bound.
A program may use at most 128 MiB of HBM per device.

v0:
```python
import math

import jax
import jax.numpy as jnp
from jax import lax
from jax.sharding import PartitionSpec as P

D = 12288
HD = 128
HALF = 6


THETA = 1000000.0
EPS = 1e-05
MASKED = -1e30


def passed_along(block, axis, distance):
    devices = range(lax.axis_size(axis))
    route = [((i - distance) % len(devices), i) for i in devices]
    return lax.ppermute(block, axis, route)


def rotate(vectors, angle_at):
    head_size = vectors.shape[-1]
    half_count = head_size // 2
    freq_index = jnp.arange(half_count, dtype=jnp.float32)
    frequency = jnp.power(THETA, -2.0 * freq_index / head_size)
    phase_angle = angle_at[..., None] * frequency
    cosine = jnp.cos(phase_angle)
    sine_part = jnp.sin(phase_angle)
    first_half = vectors[..., :half_count]
    second_half = vectors[..., half_count:]
    return jnp.concatenate(
        [
            first_half * cosine - second_half * sine_part,
            second_half * cosine + first_half * sine_part,
        ],
        -1,
    )


def shards(store, owners, positions, sel_rows, sel_hidden, norm_gain, w_query, w_keyval, w_out):
    score_scale = 1.0 / math.sqrt(HD)
    tensor_count = lax.axis_size("tensor")
    section_rank = lax.axis_index("section")
    tensor_rank = lax.axis_index("tensor")
    partner_offset = tensor_count // 2
    holds_values = tensor_rank // partner_offset
    group_rows = store.shape[1]
    kv_width = store.shape[2]
    kv_heads = kv_width // HD
    picked_rows = sel_rows.shape[1]
    query_width = w_query.shape[1]
    my_slot = lax.dynamic_index_in_dim(owners, section_rank, 0, keepdims=False)
    my_start = lax.dynamic_index_in_dim(positions, section_rank, 0, keepdims=False)
    my_rows = lax.dynamic_index_in_dim(sel_rows, section_rank, 0, keepdims=False)
    incoming_block = lax.all_gather(store, "section", axis=0, tiled=True)
    block_slots = incoming_block.shape[0]
    within = jnp.logical_and(my_slot >= 0, my_slot < block_slots)
    chosen = lax.dynamic_index_in_dim(
        incoming_block, jnp.clip(my_slot, 0, block_slots - 1), 0, keepdims=False
    )
    fetched = jnp.where(within, chosen, jnp.zeros((group_rows, kv_width), store.dtype))
    key_shift = jnp.where(holds_values == 0, my_start, 0).astype(jnp.float32)
    fetched_heads = fetched.astype(jnp.float32).reshape(group_rows, kv_heads, HD)
    shifted = rotate(fetched_heads, jnp.broadcast_to(key_shift, (group_rows, kv_heads))).astype(
        jnp.bfloat16
    )
    hidden_f32 = sel_hidden.astype(jnp.float32)
    partial_squares = jnp.sum(hidden_f32 * hidden_f32, axis=-1)
    squares = lax.psum(partial_squares, "section")
    normed = (
        hidden_f32 * lax.rsqrt(squares / D + EPS)[..., None] * norm_gain.astype(jnp.float32)
    ).astype(jnp.bfloat16)
    joined = jnp.concatenate([w_query, w_keyval], axis=1)
    projected = lax.psum_scatter(
        jnp.einsum("csd,df->csf", normed, joined, preferred_element_type=jnp.float32),
        "section",
        scatter_dimension=0,
        tiled=True,
    )[0]
    row_pos = my_start + my_rows
    query_float = row_pos.astype(jnp.float32)
    query_raw = projected[:, :query_width].reshape(picked_rows, kv_heads, HALF, HD)
    queries = rotate(
        query_raw, jnp.broadcast_to(query_float[:, None, None], (picked_rows, kv_heads, HALF))
    ).astype(jnp.bfloat16)
    fresh_raw = projected[:, query_width:].reshape(picked_rows, kv_heads, HD)
    fresh_shift = jnp.where(holds_values == 0, query_float, 0.0)
    fresh = rotate(fresh_raw, fresh_shift[:, None]).astype(jnp.bfloat16)
    patched = shifted.at[my_rows].set(fresh).reshape(group_rows, kv_width)
    blended_cache = patched[None]
    partner = passed_along(patched, "tensor", partner_offset)
    keys_local = jnp.where(holds_values == 0, patched, partner)
    values_local = jnp.where(holds_values == 0, partner, patched)
    query_rows = picked_rows * HALF
    query_mat = jnp.transpose(queries, (1, 2, 0, 3)).reshape(kv_heads, query_rows, HD)
    tiled_pos = jnp.tile(row_pos, HALF)
    start_state = (
        jnp.full((kv_heads, query_rows), MASKED, jnp.float32),
        jnp.zeros((kv_heads, query_rows), jnp.float32),
        jnp.zeros((kv_heads, query_rows, HD), jnp.float32),
    )
    key_part = lax.all_gather(keys_local, "section", axis=0, tiled=True)
    value_part = lax.all_gather(values_local, "section", axis=0, tiled=True)
    block_count = key_part.shape[0] // group_rows
    key_blocks = key_part.reshape(block_count, group_rows, kv_heads, HD)
    value_blocks = value_part.reshape(block_count, group_rows, kv_heads, HD)

    def step_block(state, inputs):
        running_max, running_total, running_sum = state
        key_block, value_block, block_number = inputs
        group_first = lax.dynamic_index_in_dim(positions, block_number, 0, keepdims=False)
        key_pos = group_first + jnp.arange(group_rows, dtype=jnp.int32)
        visible = key_pos[None, None, :] <= tiled_pos[None, :, None]
        scores = (
            jnp.einsum("gqd,kgd->gqk", query_mat, key_block, preferred_element_type=jnp.float32)
            * score_scale
        )
        scores = jnp.where(visible, scores, MASKED)
        new_max = jnp.maximum(running_max, jnp.max(scores, axis=-1))
        weights = jnp.where(visible, jnp.exp(scores - new_max[..., None]), 0.0)
        decay = jnp.exp(running_max - new_max)
        new_total = running_total * decay + jnp.sum(weights, axis=-1)
        new_sum = running_sum * decay[..., None] + jnp.einsum(
            "gqk,kgd->gqd",
            weights.astype(jnp.bfloat16),
            value_block,
            preferred_element_type=jnp.float32,
        )
        return ((new_max, new_total, new_sum), None)

    final_state = lax.scan(
        step_block,
        start_state,
        (key_blocks, value_blocks, jnp.arange(block_count, dtype=jnp.int32)),
    )[0]
    attended = (final_state[2] / final_state[1][..., None]).reshape(kv_heads, HALF, picked_rows, HD)
    attended = (
        jnp.transpose(attended, (2, 0, 1, 3)).reshape(picked_rows, query_width).astype(jnp.bfloat16)
    )
    head_block = lax.all_gather(attended[None], "section", axis=0, tiled=True)
    block_groups = head_block.shape[0]
    product = jnp.dot(
        head_block.reshape(block_groups * picked_rows, query_width),
        w_out,
        preferred_element_type=jnp.float32,
    )
    head_terms = product.reshape(block_groups, picked_rows, w_out.shape[1])
    mixed = lax.psum_scatter(
        head_terms.astype(jnp.bfloat16), "tensor", scatter_dimension=0, tiled=True
    )
    return (blended_cache, mixed)


def solution(mesh):
    return jax.shard_map(
        shards,
        mesh=mesh,
        in_specs=(
            P("section", None, "tensor"),
            P(),
            P(),
            P(),
            P(None, None, "section"),
            P("section"),
            P("section", "tensor"),
            P("section", "tensor"),
            P("tensor", "section"),
        ),
        out_specs=(P("section", None, "tensor"), P("tensor", None, "section")),
        check_vma=False,
    )
```

profile of v0, /device:TPU:36, one launch (start us, length us, event | category | flops | bytes accessed | tf_op | source)
XLA Modules:
  0.0 677.3 jit_solution(8604552064744741326)
XLA Ops:
  7.2 1.4 convert_element_type.92
  8.7 2.2 fusion.21
  10.9 47.4 %psum.7 = f32[16,96]{1,0:T(8,128)S(1)} all-reduce(f32[16,96]{1,0:T(8,128)S(1)} %fusion.21), channel_id=1, replica_groups=mesh['section'=16,'tensor'=16] {'section'}, use_global_device_ids=true, to_apply=%region_1.2 | all-reduce | flops 1536 | bytes 12288 | tf_op jit(solution)/shard_map/psum | solution.py:72
  58.3 5.9 fusion.24
  64.3 0.7 all-gather.5.cloned.1.call-update
  67.6 0.6 dynamic_slice.31
  68.9 0.7 fusion.50
  69.6 1.3 broadcast_select_fusion.4
  71.0 90.7 %reduce-scatter.3.cloned.1.call-done = f32[1,96,896]{2,1,0:T(8,128)} async-done(((f32[16,96,896]{2,1,0:T(8,128)}), f32[1,96,896]{2,1,0:T(8,128)}) %reduce-scatter.3.cloned.1.call-update) | async-done | bytes 344080 | tf_op jit(solution)/shard_map/reduce_scatter | solution.py:77
  161.6 0.8 slice_bitcast_fusion
  162.7 137.6 %all-gather.5.cloned.1.call-done = bf16[64,640,128]{2,1,0:T(8,128)(2,1)} async-done(((bf16[4,640,128]{2,1,0:T(8,128)(2,1)}), bf16[64,640,128]{2,1,0:T(8,128)(2,1)}) %all-gather.5.cloned.1.call-update) | async-done | bytes 10485776 | tf_op jit(solution)/shard_map/all_gather | solution.py:58
  300.3 0.9 bitcast_convert_fusion
  301.5 1.0 scatter_custom_fusion
  302.5 0.6 collective-permute-start
  303.2 7.1 %collective-permute-done = bf16[640,128]{1,0:T(8,128)(2,1)S(1)} collective-permute-done((bf16[640,128]{1,0:T(8,128)(2,1)S(1)}, bf16[640,128]{1,0:T(8,128)(2,1)S(1)}, u32[]{:S(2)}, u32[]{:S(2)}) %collective-permute-start) | collective-permute-done | bytes 163872 | tf_op jit(solution)/shard_map/ppermute | solution.py:21
  310.3 0.8 broadcast_select_fusion.2
  311.7 1.3 add_bitcast_fusion
  313.7 57.8 %all-gather.7.cloned.1.call-done = bf16[10240,128]{1,0:T(8,128)(2,1)} async-done(((bf16[640,128]{1,0:T(8,128)(2,1)}), bf16[10240,128]{1,0:T(8,128)(2,1)}) %all-gather.7.cloned.1.call-update) | async-done | bytes 2621456 | tf_op jit(solution)/shard_map/all_gather | solution.py:105
  371.5 63.5 %all-gather.9.cloned.1.call-done = bf16[10240,128]{1,0:T(8,128)(2,1)} async-done(((bf16[640,128]{1,0:T(8,128)(2,1)}), bf16[10240,128]{1,0:T(8,128)(2,1)}) %all-gather.9.cloned.1.call-update) | async-done | bytes 2621456 | tf_op jit(solution)/shard_map/all_gather | solution.py:106
  435.1 112.2 %while.15 = (s32[]{:T(128)}, f32[1,576]{1,0:T(1,128)S(1)}, f32[1,576]{1,0:T(1,128)S(1)}, f32[1,576,128]{2,1,0:T(8,128)S(1)}, s32[16]{0:T(128)S(1)}, /*index=5*/s...) while((s32[]{:T(128)}, f32[1,576]{1,0:T(1,128)S(1)}, ...), condition=%wide.region_7.8_spmd.clone, body=%wide.region_4.7_spmd.clone.sunk | while | flops 193392640 | bytes 5552471 | solution.py:134
  437.5 0.6 dynamic_slice.63
  438.6 1.4 fusion.63
  440.6 1.4 fusion.67
  444.5 0.6 dynamic_slice.63
  445.6 1.4 fusion.63
  447.6 1.4 fusion.67
  451.5 0.6 dynamic_slice.63
  452.7 1.4 fusion.63
  454.6 1.4 fusion.67
  458.5 0.6 dynamic_slice.63
  459.7 1.4 fusion.63
  461.6 1.4 fusion.67
  465.5 0.6 dynamic_slice.63
  466.7 1.4 fusion.63
  468.7 1.4 fusion.67
  472.5 0.6 dynamic_slice.63
  473.7 1.4 fusion.63
  475.7 1.4 fusion.67
  479.5 0.6 dynamic_slice.63
  480.7 1.4 fusion.63
  482.7 1.4 fusion.67
  486.6 0.6 dynamic_slice.63
  487.7 1.4 fusion.63
  489.7 1.4 fusion.67
  494.7 1.4 fusion.63
  496.7 1.4 fusion.67
  501.8 1.4 fusion.63
  503.7 1.4 fusion.67
  508.8 1.4 fusion.63
  510.8 1.4 fusion.67
  515.8 1.4 fusion.63
  517.8 1.4 fusion.67
  522.8 1.4 fusion.63
  524.8 1.4 fusion.67
  529.8 1.4 fusion.63
  531.8 1.4 fusion.67
  536.8 1.4 fusion.63
  538.8 1.4 fusion.67
  543.8 1.4 fusion.63
  545.8 1.4 fusion.67
  547.5 0.8 convert_element_type.99
  548.5 59.4 %all-gather.11.cloned.1.call-done = bf16[16,96,768]{2,1,0:T(8,128)(2,1)} async-done(((bf16[1,96,768]{2,1,0:T(8,128)(2,1)}), bf16[16,96,768]{2,1,0:T(8,128)(2,1)}) %all-gather.11.cloned.1.call-update) | async-done | bytes 2359312 | tf_op jit(solution)/shard_map/all_gather | solution.py:143
  607.9 5.1 convolution_convert_fusion
  613.0 57.5 %reduce-scatter.5.cloned.1.call-done = bf16[1,96,768]{2,1,0:T(8,128)(2,1)} async-done(((bf16[16,96,768]{2,1,0:T(8,128)(2,1)}), bf16[1,96,768]{2,1,0:T(8,128)(2,1)}) %reduce-scatter.5.cloned.1.call-update) | async-done | bytes 147472 | tf_op jit(solution)/shard_map/reduce_scatter | solution.py:151
  (178 shorter events, 35.9 us)
Async XLA Ops:
  7.2 600.7 %copy-start = (bf16[768,768]{1,0:T(8,128)(2,1)S(1)}, bf16[768,768]{1,0:T(8,128)(2,1)}, u32[]{:S(2)}) copy-start(bf16[768,768]{1,0:T(8,128)(2,1)} %param.19) | copy-start | bytes 3538948
  7.2 51.1 %copy-start.1 = (bf16[16,96,768]{2,1,0:T(8,128)(2,1)S(1)}, bf16[16,96,768]{2,1,0:T(8,128)(2,1)}, u32[]{:S(2)}) copy-start(bf16[16,96,768]{2,1,0:T(8,128)(2,1)} %param.15) | copy-start | bytes 7077892
  7.2 154.4 %reduce-scatter.3.cloned.1.call-start = ((), (), s32[]{:S(2)}) async-start(), calls=%async_computation.3 | async-start | bytes 5849088 | tf_op jit(solution)/shard_map/reduce_scatter | solution.py:77
  64.2 0.8 copy-start.4
  64.2 3.4 copy-start.5
  64.2 236.0 %all-gather.5.cloned.1.call-start = ((), (), s32[]{:S(2)}) async-start(), calls=%async_computation.2 | async-start | bytes 11141120 | tf_op jit(solution)/shard_map/all_gather | solution.py:58
  65.0 306.6 %all-gather.7.cloned.1.call-start = ((), (), s32[]{:S(2)}) async-start(), calls=%async_computation.4 | async-start | bytes 2785280 | tf_op jit(solution)/shard_map/all_gather | solution.py:105
  301.2 11.9 %copy-start.3 = (f32[1,96,896]{2,1,0:T(8,128)S(1)}, f32[1,96,896]{2,1,0:T(8,128)}, u32[]{:S(2)}) copy-start(f32[1,96,896]{2,1,0:T(8,128)} %reduce-scatter.3.cloned.1.call-done) | copy-start | bytes 1032196
  302.5 11.0 %copy-start.2 = (bf16[640,128]{1,0:T(8,128)(2,1)}, bf16[640,128]{1,0:T(8,128)(2,1)S(1)}, u32[]{:S(2)}) copy-start(bf16[640,128]{1,0:T(8,128)(2,1)S(1)} %scatter_custom_fusion) | copy-start | bytes 491524
  302.5 7.7 %collective-permute-start = (bf16[640,128]{1,0:T(8,128)(2,1)S(1)}, bf16[640,128]{1,0:T(8,128)(2,1)S(1)}, u32[]{:S(2)}, u32[]{:S(2)}) collective-permute-start(bf16[640,128]{1,0:T(8,128)(2,1)S(1)} %scatter_custom_fusion), channel_id=1, source_target_pairs={{8,0},{9,1},{10,2},{11,3},{12,4},{13,5},{14,6},{15,7},{0,8},{1,9},... | collective-permute-start | bytes 491528 | tf_op jit(solution)/shard_map/ppermute | solution.py:21
  311.1 124.0 %all-gather.9.cloned.1.call-start = ((), (), s32[]{:S(2)}) async-start(), calls=%async_computation.5 | async-start | bytes 2785280 | tf_op jit(solution)/shard_map/all_gather | solution.py:106
  311.6 296.2 %all-gather.11.cloned.1.call-start = ((), (), s32[]{:S(2)}) async-start(), calls=%async_computation.6 | async-start | bytes 2506752 | tf_op jit(solution)/shard_map/all_gather | solution.py:143
  548.4 122.1 %reduce-scatter.5.cloned.1.call-start = ((), (), s32[]{:S(2)}) async-start(), calls=%async_computation.7 | async-start | bytes 2506752 | tf_op jit(solution)/shard_map/reduce_scatter | solution.py:151
Sparse Core Ops, SparseCore 0:
  64.3 97.2 reduce-scatter.2
  164.1 136.1 all-gather.4
  311.2 60.2 all-gather.6
  373.9 61.1 all-gather.8
  548.5 59.2 all-gather.10
  613.1 57.3 reduce-scatter.4
where the time goes:
time: 690 us; the launch traced here: 677 us
  waiting for transfers between devices  475 us (69%)
  matrix products  57 us (8%)
  blocking collectives  47.4 us (7%)
  loops' own time  28.5 us (4%)
  other arithmetic  28.3 us (4%)
  local copies, waits for them, and re-layouts  23.4 us (3%)
  between operations  16.9 us (2%)
    all_gather x1, waiting for transfers between devices, shards(): incoming_block = lax.all_gather(store, 'section', axis=0, tiled=True)  138 us
    reduce_scatter x1, waiting for transfers between devices, shards(): lax.psum_scatter(jnp.einsum('csd,df->csf', normed, joined, preferred_elem...  90.7 us
    all_gather x1, waiting for transfers between devices, shards(): value_part = lax.all_gather(values_local, 'section', axis=0, tiled=True)  63.5 us
    all_gather x1, waiting for transfers between devices, shards(): head_block = lax.all_gather(attended[None], 'section', axis=0, tiled=True)  59.4 us
    all_gather x1, waiting for transfers between devices, shards(): key_part = lax.all_gather(keys_local, 'section', axis=0, tiled=True)  57.8 us
    reduce_scatter x1, waiting for transfers between devices, shards(): lax.psum_scatter(head_terms.astype(jnp.bfloat16), 'tensor', scatter_dimen...  57.5 us
    psum x1, blocking collectives, shards(): squares = lax.psum(partial_squares, 'section')  47.4 us
    another operation x1, loops' own time, shards(): lax.scan(step_block, start_state, (key_blocks, value_blocks, jnp.arange(b...  28.5 us
  transfers between devices with their start and end apart: 7, of which 7 were waited for; matrix products, arithmetic and copies ran while one was open for 1% of the time, Pallas kernels for 0%

commit v1 on v0

v1 whole, which is shorter than its diff:
```python
import math

import jax
import jax.numpy as jnp
from jax import lax
from jax.experimental import pallas as pl
from jax.experimental.pallas import tpu as pltpu
from jax.sharding import PartitionSpec as P

D = 12288
HD = 128
HALF = 6
L = 640
SEL = 96
THETA = 1000000.0
EPS = 1e-05
MASKED = -1e30
MESH = pl.DeviceIdType.MESH
F32 = jnp.float32
BF16 = jnp.bfloat16
QW = 768
PW = 896
QPAD = 640
SCALE2 = math.log2(math.e) / math.sqrt(HD)


def along(section=None, tensor=None):
    where = {}
    if section is not None:
        where["section"] = section
    if tensor is not None:
        where["tensor"] = tensor
    return where


def greet(peers):
    barrier = pltpu.get_barrier_semaphore()
    for peer in peers:
        pl.semaphore_signal(barrier, inc=1, device_id=peer, device_id_type=MESH)
    pl.semaphore_wait(barrier, len(peers))


def spread(vec, lanes):
    return lax.dot_general(
        vec, jnp.ones((8, lanes), F32), (((0,), (0,)), ((), ())),
        precision=lax.Precision.HIGHEST, preferred_element_type=F32,
    )


def front(owners, h, gain, wq, wkv, store, trig, rows,
          blended, kv, q,
          stbuf, stsend, strecv, p2, p2r, acc, psend, precv, zsend, zrecv,
          sqs, sqr, sqz, sqzr, fresh, ssem, rsem):
    s = lax.axis_index("section")
    t = lax.axis_index("tensor")
    y, z = s // 4, s % 4
    kind = t // 8

    def ypeer(d):
        return along(section=((y + d) % 4) * 4 + z)

    def zpeer(d):
        return along(section=y * 4 + (z + d) % 4)

    partner = along(tensor=(t + 8) % 16)
    sent = []

    def push(i, src, dst, dev):
        c = pltpu.make_async_remote_copy(
            src_ref=src, dst_ref=dst, send_sem=ssem.at[i], recv_sem=rsem.at[i],
            device_id=dev, device_id_type=MESH)
        c.start()
        sent.append(c)
        return c

    greet([ypeer(1), ypeer(2), ypeer(3), zpeer(1), zpeer(2), zpeer(3), partner])

    st_up = push(0, store, stbuf.at[y], ypeer(1))
    st_dn = push(1, store, stbuf.at[y], ypeer(3))

    ones8 = jnp.ones((8, 128), F32)

    def multiply(d, out, i):
        hf = h[pl.ds(((y + d) % 4) * 4, 4)].astype(F32).reshape(384, 768)
        hg = (hf * gain[...].astype(F32)).astype(BF16)
        a = jnp.dot(hg, wq[...], preferred_element_type=F32)
        b = jnp.dot(hg, wkv[...], preferred_element_type=F32)
        out[i, :, :, :QW] = a.reshape(4, SEL, QW).astype(out.dtype)
        out[i, :, :, QW:] = b.reshape(4, SEL, HD).astype(out.dtype)
        sq = hf * hf
        part = sq[:, :128]
        for k in range(1, 6):
            part = part + sq[:, k * 128:(k + 1) * 128]
        sqs[d] = jnp.zeros((8, 128), F32)
        for g in range(4):
            row = lax.dot_general(
                ones8, part[g * SEL:(g + 1) * SEL], (((1,), (1,)), ((), ())),
                precision=lax.Precision.HIGHEST, preferred_element_type=F32)
            sqs[d, g:g + 1, :SEL] = row[:1]

    multiply(2, p2, 0)
    up2 = push(2, p2.at[0, pl.ds(0, 2)], p2r.at[0], ypeer(1))
    dn2 = push(3, p2.at[0, pl.ds(2, 2)], p2r.at[1], ypeer(3))
    sq_y = [push(8, sqs.at[2], sqr.at[2], ypeer(2))]
    multiply(1, acc, 1)
    sq_y.append(push(9, sqs.at[1], sqr.at[3], ypeer(1)))
    multiply(3, acc, 2)
    sq_y.append(push(10, sqs.at[3], sqr.at[1], ypeer(3)))
    multiply(0, acc, 0)
    stbuf[y] = store[...]

    up2.wait_recv()
    psend[0, :2] = (acc[1, :2] + p2r[0].astype(F32)).astype(BF16)
    psend[0, 2:] = acc[1, 2:].astype(BF16)
    up1 = push(4, psend.at[0], precv.at[0], ypeer(1))
    dn2.wait_recv()
    psend[1, 2:] = (acc[2, 2:] + p2r[1].astype(F32)).astype(BF16)
    psend[1, :2] = acc[2, :2].astype(BF16)
    dn1 = push(5, psend.at[1], precv.at[1], ypeer(3))

    st_up.wait_recv()
    below = (y + 3) % 4
    above = (y + 1) % 4
    st_up2 = push(6, stbuf.at[below, pl.ds(0, 2)], stbuf.at[below, pl.ds(0, 2)], ypeer(1))
    st_dn.wait_recv()
    st_dn2 = push(7, stbuf.at[above, pl.ds(2, 2)], stbuf.at[above, pl.ds(2, 2)], ypeer(3))

    for c in sq_y:
        c.wait_recv()
    sqz[...] = sqs[0] + sqr[1] + sqr[2] + sqr[3]
    sq_z = [push(11 + d, sqz, sqzr.at[4 - d], zpeer(d)) for d in (1, 2, 3)]

    st_up2.wait_recv()
    st_dn2.wait_recv()

    def picked(d):
        slot = owners[y * 4 + (z + d) % 4]
        here = ((slot >> 2) & 3) == z
        block = stbuf[slot >> 4, slot & 3]
        return jnp.where(here, block, jnp.zeros_like(block))

    st_z = []
    for d in (2, 1, 3):
        stsend[d] = picked(d)
        st_z.append(push(15 + d, stsend.at[d], strecv.at[4 - d], zpeer(d)))

    up1.wait_recv()
    dn1.wait_recv()
    total = acc.at[0]
    pr_z = []
    for d in (2, 1, 3):
        g = (z + d) % 4
        zsend[d] = (total[g] + precv[0, g].astype(F32) + precv[1, g].astype(F32)).astype(BF16)
        pr_z.append(push(19 + d, zsend.at[d], zrecv.at[4 - d], zpeer(d)))

    for c in sq_z:
        c.wait_recv()
    squares = sqz[...] + sqzr[1] + sqzr[2] + sqzr[3]
    mine = lax.broadcasted_iota(jnp.int32, (8, 128), 0) == z
    squares = spread(jnp.where(mine, squares, 0.0), 128)[:SEL]
    inv = lax.rsqrt(squares / D + EPS)

    for c in pr_z:
        c.wait_recv()
    cos = trig[0, :SEL]
    sin = trig[1, :SEL]

    def summed(lo):
        cols = pl.ds(lo, HD)
        v = total[z, :, cols] + precv[0, z, :, cols].astype(F32)
        v = v + precv[1, z, :, cols].astype(F32)
        for d in (1, 2, 3):
            v = v + zrecv[d, :, cols].astype(F32)
        return v * inv

    def turned(v, c, sn):
        return v * c + pltpu.roll(v, 64, 1) * sn

    for j in range(HALF):
        q[0, j * SEL:(j + 1) * SEL] = turned(summed(j * HD), cos, sin).astype(BF16)
    q_y = [push(27 + d, q.at[0, pl.ds(0, 576)], q.at[4 - d, pl.ds(0, 576)], ypeer(d))
           for d in (2, 1, 3)]
    for r in range(4):
        q[r, 576:] = jnp.zeros((QPAD - 576, HD), BF16)

    values = kind == 1
    fresh[...] = jnp.zeros_like(fresh)
    fresh[:SEL] = turned(
        summed(QW), jnp.where(values, 1.0, cos), jnp.where(values, 0.0, sin)).astype(BF16)

    cached = picked(0)
    for c in st_z:
        c.wait_recv()
    for d in (1, 2, 3):
        cached = cached + strecv[d]
    shift_cos = jnp.where(values, 1.0, trig[0, SEL:SEL + 1])
    shift_sin = jnp.where(values, 0.0, trig[1, SEL:SEL + 1])
    shifted = turned(cached.astype(F32), shift_cos, shift_sin).astype(BF16)
    hit = lax.broadcasted_iota(jnp.int32, (L, 128), 0) == rows[...]
    hot = jnp.where(hit, 1.0, 0.0)
    placed = jnp.dot(hot.astype(BF16), fresh[...], preferred_element_type=F32)
    patched = jnp.where(jnp.max(hot, axis=1, keepdims=True) > 0.0, placed, shifted.astype(F32))
    patched = patched.astype(BF16)
    blended[...] = patched
    kv[kind, 0] = patched
    kv_z = [push(31 + d, kv.at[kind, 0], kv.at[kind, 4 - d], zpeer(d)) for d in (2, 1, 3)]
    kv_x = [push(35, kv.at[kind, 0], kv.at[kind, 0], partner)]
    for d, c in zip((2, 1, 3), kv_z):
        c.wait_recv()
        r = 4 - d
        kv_x.append(push(35 + r, kv.at[kind, r], kv.at[kind, r], partner))
    for c in kv_x:
        c.wait_recv()
    for c in q_y:
        c.wait_recv()
    for c in sent:
        c.wait_send()


def attend(positions, q, kv, limit, o, lse, sbuf, pbuf):
    s = lax.axis_index("section")
    y, z = s // 4, s % 4

    def tile(i, carry):
        cols = pl.ds(pl.multiple_of(i * 256, 256), 256)
        lane = i * 256 + lax.broadcasted_iota(jnp.int32, (1, 256), 1)
        first = jnp.full((1, 256), positions[y * 4 + z], jnp.int32)
        for d in (1, 2, 3):
            first = jnp.where(lane >= d * QPAD, positions[((y + d) % 4) * 4 + z], first)
        block = q[cols]
        lim = limit[:, cols]
        top = jnp.full((1, 256), MASKED, F32)
        hidden = []
        for e in range(4):
            sc = lax.dot_general(
                kv[0, e], block, (((1,), (1,)), ((), ())), preferred_element_type=F32)
            if e == 0:
                sc = jnp.where(lax.broadcasted_iota(jnp.int32, (L, 256), 0) <= lim, sc, MASKED)
            sbuf[e] = sc
            hid = positions[y * 4 + (z + e) % 4] > first
            hidden.append(hid)
            top = jnp.maximum(
                top, jnp.where(hid, MASKED, jnp.max(sc, axis=0, keepdims=True)))
        top = top * SCALE2
        weight = jnp.zeros((1, 256), F32)
        for e in range(4):
            base = top + jnp.where(hidden[e], 1e30, 0.0)
            p = jnp.exp2(sbuf[e] * SCALE2 - base)
            weight = weight + jnp.sum(p, axis=0, keepdims=True)
            pbuf[e] = p.astype(BF16)
        num = lax.dot_general(
            kv[1].reshape(4 * L, HD), pbuf[...].reshape(4 * L, 256), (((0,), (0,)), ((), ())),
            preferred_element_type=F32)
        some = weight > 0.0
        safe = jnp.where(some, weight, 1.0)
        o[cols] = (num * (1.0 / safe)).T.astype(BF16)
        lse[:, cols] = jnp.broadcast_to(
            jnp.where(some, top + jnp.log2(safe), MASKED), (8, 256))
        return carry

    lax.fori_loop(0, 4 * QPAD // 256, tile, 0)


def back(o, lse, w, out,
         orecv, lrecv, ag, prod, crecv, csum, xrecv, zlsend, zlrecv, ssem, rsem):
    s = lax.axis_index("section")
    t = lax.axis_index("tensor")
    y, z = s // 4, s % 4
    x, zl, core = t // 4, (t // 2) % 2, t % 2

    def ypeer(d):
        return along(section=((y + d) % 4) * 4 + z)

    def zpeer(d):
        return along(section=y * 4 + (z + d) % 4)

    def xpeer(d):
        return along(tensor=((x + d) % 4) * 4 + t % 4)

    twin = along(tensor=x * 4 + zl * 2 + 1 - core)
    pair = along(tensor=x * 4 + (1 - zl) * 2 + core)
    sent = []

    def make(i, src, dst, dev, r=None):
        return pltpu.make_async_remote_copy(
            src_ref=src, dst_ref=dst, send_sem=ssem.at[i],
            recv_sem=rsem.at[i if r is None else r],
            device_id=dev, device_id_type=MESH)

    def push(i, src, dst, dev):
        c = make(i, src, dst, dev)
        c.start()
        sent.append(c)
        return c

    greet([ypeer(1), ypeer(2), ypeer(3), zpeer(1), zpeer(2), zpeer(3),
           xpeer(1), xpeer(2), xpeer(3), twin, pair])

    got = []
    for d in (2, 1, 3):
        got.append(push(d, o.at[d, pl.ds(0, 576)], orecv.at[4 - d], ypeer(d)))
        got.append(push(3 + d, lse.at[:, pl.ds(d * QPAD, QPAD)], lrecv.at[4 - d], ypeer(d)))
    for c in got:
        c.wait_recv()
    logs = [lse[:1, :QPAD]] + [lrecv[d, :1] for d in (1, 2, 3)]
    top = jnp.maximum(jnp.maximum(logs[0], logs[1]), jnp.maximum(logs[2], logs[3]))
    share = [jnp.exp2(v - top) for v in logs]
    whole = share[0] + share[1] + share[2] + share[3]
    line = lax.broadcasted_iota(jnp.int32, (8, QPAD), 0) == 0
    merged = jnp.zeros((576, HD), F32)
    for d in range(4):
        part = o[0, :576] if d == 0 else orecv[d]
        col = spread(jnp.where(line, share[d] / whole, 0.0), HD)[:576]
        merged = merged + part.astype(F32) * col
    for j in range(HALF):
        ag[0, z, :, j * HD:(j + 1) * HD] = merged[j * SEL:(j + 1) * SEL].astype(BF16)

    def grp(d):
        return (z + d) % 4

    zs = {d: push(6 + d, ag.at[0, z], ag.at[0, z], zpeer(d)) for d in (2, 1, 3)}
    ups, dns = {}, {}
    for d in (0, 1, 3, 2):
        if d:
            zs[4 - d].wait_recv()
        ups[d] = push(10 + d, ag.at[0, grp(d)], ag.at[3, grp(d)], ypeer(1))
        dns[d] = push(14 + d, ag.at[0, grp(d)], ag.at[1, grp(d)], ypeer(3))

    def multiply(r):
        a = jnp.dot(ag[r].reshape(384, 768), w[...], preferred_element_type=F32)
        a = a.reshape(4, SEL, 768).astype(BF16)
        for g in range(4):
            prod[r, g % 2, g // 2] = a[g]
        return push(22 + r, prod.at[r, 1 - core], crecv.at[r], twin)

    def send_x(r, c):
        c.wait_recv()
        csum[r] = (prod[r, core].astype(F32) + crecv[r].astype(F32)).astype(BF16)
        d = (y + r + 4 - x) % 4

        @pl.when(d != 0)
        def _():
            make(26 + r, csum.at[r], xrecv.at[(4 - d) % 4], xpeer(d), 30 + (4 - d) % 4).start()

    tw0 = multiply(0)
    fw_up, fw_dn = {}, {}
    for d in (0, 1, 3, 2):
        ups[d].wait_recv()
        dns[d].wait_recv()
        if d in (0, 1):
            fw_up[d] = push(18 + d, ag.at[3, grp(d)], ag.at[2, grp(d)], ypeer(1))
        else:
            fw_dn[d] = push(18 + d, ag.at[1, grp(d)], ag.at[2, grp(d)], ypeer(3))
    send_x(0, tw0)
    tw1 = multiply(1)
    tw3 = multiply(3)
    send_x(1, tw1)
    send_x(3, tw3)
    for d in (0, 1):
        fw_up[d].wait_recv()
    for d in (3, 2):
        fw_dn[d].wait_recv()
    tw2 = multiply(2)
    send_x(2, tw2)

    for d in (1, 2, 3):
        make(26, csum.at[0], xrecv.at[d], xpeer(d), 30 + d).wait_recv()
    own = (x + 4 - y) % 4

    def reduced(k):
        v = csum[own, k].astype(F32)
        for d in (1, 2, 3):
            v = v + xrecv[d, k].astype(F32)
        return v

    zlsend[...] = reduced(1 - zl).astype(BF16)
    last = push(34, zlsend, zlrecv, pair)
    keep = reduced(zl)
    last.wait_recv()
    out[...] = (keep + zlrecv[...].astype(F32)).astype(BF16)
    for r in range(4):
        @pl.when((y + r + 4 - x) % 4 != 0)
        def _():
            make(26 + r, csum.at[r], xrecv.at[1], xpeer(1), 31).wait_send()
    for c in sent:
        c.wait_send()


VM = pl.BlockSpec(memory_space=pltpu.VMEM)
SM = pl.BlockSpec(memory_space=pltpu.SMEM)


def shards(store, owners, positions, sel_rows, sel_hidden, norm_gain, w_query, w_keyval, w_out):
    section = lax.axis_index("section")
    my_start = lax.dynamic_index_in_dim(positions, section, 0, keepdims=False)
    my_rows = lax.dynamic_index_in_dim(sel_rows, section, 0, keepdims=False)
    where = jnp.concatenate([my_start + my_rows, jnp.full((8,), my_start)]).astype(F32)
    freq_index = jnp.arange(HD // 2, dtype=F32)
    frequency = jnp.power(THETA, -2.0 * freq_index / HD)
    angle = where[:, None] * frequency
    cos, sin = jnp.cos(angle), jnp.sin(angle)
    trig = jnp.stack([jnp.concatenate([cos, cos], 1), jnp.concatenate([-sin, sin], 1)])
    rows = jnp.concatenate([my_rows, jnp.full((128 - SEL,), -1, jnp.int32)])[None]
    limit = jnp.concatenate(
        [jnp.tile(my_rows, HALF), jnp.full((4 * QPAD - 576,), L, jnp.int32)])[None]

    blended, kv, q = pl.pallas_call(
        front,
        name="front",
        out_shape=(
            jax.ShapeDtypeStruct((L, HD), BF16),
            jax.ShapeDtypeStruct((2, 4, L, HD), BF16),
            jax.ShapeDtypeStruct((4, QPAD, HD), BF16),
        ),
        in_specs=[SM] + [VM] * 7,
        out_specs=(VM, VM, VM),
        scratch_shapes=[
            pltpu.VMEM((4, 4, L, HD), BF16),
            pltpu.VMEM((4, L, HD), BF16),
            pltpu.VMEM((4, L, HD), BF16),
            pltpu.VMEM((1, 4, SEL, PW), BF16),
            pltpu.VMEM((2, 2, SEL, PW), BF16),
            pltpu.VMEM((3, 4, SEL, PW), F32),
            pltpu.VMEM((2, 4, SEL, PW), BF16),
            pltpu.VMEM((2, 4, SEL, PW), BF16),
            pltpu.VMEM((4, SEL, PW), BF16),
            pltpu.VMEM((4, SEL, PW), BF16),
            pltpu.VMEM((4, 8, 128), F32),
            pltpu.VMEM((4, 8, 128), F32),
            pltpu.VMEM((8, 128), F32),
            pltpu.VMEM((4, 8, 128), F32),
            pltpu.VMEM((128, HD), BF16),
            pltpu.SemaphoreType.DMA((39,)),
            pltpu.SemaphoreType.DMA((39,)),
        ],
        compiler_params=pltpu.CompilerParams(
            collective_id=0, has_side_effects=True, vmem_limit_bytes=56 * 2**20),
    )(owners, sel_hidden, norm_gain[None], w_query, w_keyval, store, trig, rows)

    o, lse = pl.pallas_call(
        attend,
        name="attend",
        out_shape=(
            jax.ShapeDtypeStruct((4 * QPAD, HD), BF16),
            jax.ShapeDtypeStruct((8, 4 * QPAD), F32),
        ),
        in_specs=[SM] + [VM] * 3,
        out_specs=(VM, VM),
        scratch_shapes=[
            pltpu.VMEM((4, L, 256), F32),
            pltpu.VMEM((4, L, 256), BF16),
        ],
        compiler_params=pltpu.CompilerParams(vmem_limit_bytes=56 * 2**20),
    )(positions, q.reshape(4 * QPAD, HD), kv, limit)

    mixed = pl.pallas_call(
        back,
        name="back",
        out_shape=jax.ShapeDtypeStruct((SEL, 768), BF16),
        in_specs=[VM] * 3,
        out_specs=VM,
        scratch_shapes=[
            pltpu.VMEM((4, 576, HD), BF16),
            pltpu.VMEM((4, 8, QPAD), F32),
            pltpu.VMEM((4, 4, SEL, 768), BF16),
            pltpu.VMEM((4, 2, 2, SEL, 768), BF16),
            pltpu.VMEM((4, 2, SEL, 768), BF16),
            pltpu.VMEM((4, 2, SEL, 768), BF16),
            pltpu.VMEM((4, 2, SEL, 768), BF16),
            pltpu.VMEM((SEL, 768), BF16),
            pltpu.VMEM((SEL, 768), BF16),
            pltpu.SemaphoreType.DMA((35,)),
            pltpu.SemaphoreType.DMA((35,)),
        ],
        compiler_params=pltpu.CompilerParams(
            collective_id=1, has_side_effects=True, vmem_limit_bytes=56 * 2**20),
    )(o.reshape(4, QPAD, HD), lse, w_out)
    return blended[None], mixed[None]


def solution(mesh):
    return jax.shard_map(
        shards,
        mesh=mesh,
        in_specs=(
            P("section", None, "tensor"),
            P(),
            P(),
            P(),
            P(None, None, "section"),
            P("section"),
            P("section", "tensor"),
            P("section", "tensor"),
            P("tensor", "section"),
        ),
        out_specs=(P("section", None, "tensor"), P("tensor", None, "section")),
        check_vma=False,
    )
```

time: 690 us -> 211 us (0.31); the launches traced: 677 us -> 210 us
  waiting for transfers between devices: 475 us -> 0 us
  Pallas kernels: 0 us -> 200 us
  matrix products: 57 us -> 0 us
  blocking collectives: 47.4 us -> 0 us
  loops' own time: 28.5 us -> 0 us
  other arithmetic: 28.3 us -> 3.02 us
  local copies, waits for them, and re-layouts: 23.4 us -> 5.97 us
  between operations: 16.9 us -> 0.69 us
    all_gather x4 -> x0, waiting for transfers between devices: 318 us -> none  [the longest x1 138 us: shards(): incoming_block = lax.all_gather(store, 'section', axis=0, tiled=True)]
    pallas_call x0 -> x3, Pallas kernels: none -> 200 us  [the longest x1 111 us: shards(): pl.pallas_call(front, name='front', out_shape=(jax.ShapeDtypeStruct((L, H...]
    reduce_scatter x2 -> x0, waiting for transfers between devices: 148 us -> none  [the longest x1 90.7 us: shards(): lax.psum_scatter(jnp.einsum('csd,df->csf', normed, joined, preferred_elem...]
    dot_general x34 -> x0, matrix products: 57 us -> none  [the longest x16 23.1 us: step_block(): jnp.einsum('gqk,kgd->gqd', weights.astype(jnp.bfloat16), value_block, pre...]
    psum x1 -> x0, blocking collectives: 47.4 us -> none  [shards(): squares = lax.psum(partial_squares, 'section')]
    another operation x1 -> x0, loops' own time: 28.5 us -> none  [shards(): lax.scan(step_block, start_state, (key_blocks, value_blocks, jnp.arange(b...]
    dynamic_slice x34 -> x1, local copies, waits for them, and re-layouts: 20.1 us -> 1.24 us  [shards(): my_start = lax.dynamic_index_in_dim(positions, section, 0, keepdims=False)]
    reduce_sum x17 -> x0, other arithmetic: 9.86 us -> none  [the longest x16 7.64 us: step_block(): new_total = running_total * decay + jnp.sum(weights, axis=-1)]
  transfers between devices with their start and end apart: 7 -> 0, of which waited for: 7 -> 0; matrix products, arithmetic and copies ran while one was open for 1% -> 0% of each run, Pallas kernels for 0% -> 0%
where the time goes in v1:
time: 211 us; the launch traced here: 210 us
  Pallas kernels  200 us (95%)
  local copies, waits for them, and re-layouts  5.97 us (3%)
  other arithmetic  3.02 us (1%)
    pallas_call x1, Pallas kernels, shards(): pl.pallas_call(front, name='front', out_shape=(jax.ShapeDtypeStruct((L, H...  111 us
    pallas_call x1, Pallas kernels, shards(): pl.pallas_call(back, name='back', out_shape=jax.ShapeDtypeStruct((SEL, 76...  70.6 us
    pallas_call x1, Pallas kernels, shards(): pl.pallas_call(attend, name='attend', out_shape=(jax.ShapeDtypeStruct((4...  18.9 us

profile of v1, /device:TPU:36, one launch (start us, length us, event | category | flops | bytes accessed | tf_op | source)
XLA Modules:
  0.0 209.9 jit_solution(16286704466985852036)
XLA Ops:
  0.6 1.2 dynamic_slice.8
  1.9 1.3 broadcast_add_fusion
  3.2 0.6 pad_convert_fusion
  3.9 0.5 pad_bitcast_fusion.rows
  4.4 1.3 broadcast_in_dim.20.gain
  5.7 0.1 tile.10
  5.8 0.6 broadcast_in_dim.23.limit
  6.4 0.3 multiply_cosine_fusion
  6.6 0.1 maximum_bitcast_fusion
  6.7 0.7 pad_maximum_fusion.trig
  7.4 110.7 %front.1 = (bf16[640,128]{1,0:T(8,128)(2,1)}, bf16[2,4,640,128]{3,2,1,0:T(8,128)(2,1)}, bf16[4,640,128]{2,1,0:T(8,128)(2,1)}) custom-call(s32[16]{0:T(128)} %owners.1, bf16[16,96,768]{2,1,0:T(8,128)(2,1)} %h.1, bf16[1,768]{1,0:T(2,128)(2,1)} %broadcast_in_dim.20.gain, bf16[768,768]{1,0:T(8,128)(2,1)} %wq.1, bf16[768,128]{1,0:T(8,128)(2,1)} %wkv.1, ...), custom_call_target="tpu_custom_call" | custom-call | tf_op jit(solution)/shard_map/front/pallas_call | solution.py:407
  118.1 18.9 %attend.1 = (bf16[2560,128]{1,0:T(8,128)(2,1)}, f32[8,2560]{1,0:T(8,128)}) custom-call(s32[16]{0:T(128)} %positions.1, bf16[2560,128]{1,0:T(8,128)(2,1)} %bitcast.14, bf16[2,4,640,128]{3,2,1,0:T(8,128)(2,1)} %get-tuple-element.9.kv, s32[1,2560]{1,0:T(1,128)} %broadcast_in_dim.23.limit), custom_call_target="tpu_custom_call" | custom-call | tf_op jit(solution)/shard_map/attend/pallas_call | solution.py:440
  137.0 0.0 copy-start
  137.0 70.6 %back.1 = bf16[96,768]{1,0:T(8,128)(2,1)} custom-call(bf16[4,640,128]{2,1,0:T(8,128)(2,1)} %bitcast.15, f32[8,2560]{1,0:T(8,128)} %get-tuple-element.11.lse, bf16[768,768]{1,0:T(8,128)(2,1)} %w.1), custom_call_target="tpu_custom_call" | custom-call | tf_op jit(solution)/shard_map/back/pallas_call | solution.py:456
  207.7 0.0 copy-done
  207.7 0.7 copy.13
  208.4 1.6 copy.14
  (3 shorter events, 0.0 us)
Async XLA Ops:
  137.0 70.7 %copy-start = (bf16[640,128]{1,0:T(8,128)(2,1)S(1)}, bf16[640,128]{1,0:T(8,128)(2,1)}, u32[]{:S(2)}) copy-start(bf16[640,128]{1,0:T(8,128)(2,1)} %get-tuple-element.7) | copy-start | bytes 491524

commit v2 on v0

v2 whole, which is shorter than its diff:
```python
import math

import jax
import jax.numpy as jnp
import numpy as np
from jax import lax
from jax.experimental import pallas as pl
from jax.experimental.pallas import tpu as pltpu
from jax.sharding import PartitionSpec as P

D = 12288
HD = 128
HALF = 6
L = 640
LH = L // 2
SEL = 96
THETA = 1000000.0
EPS = 1e-05
MASKED = -1e30
MESH = pl.DeviceIdType.MESH
F32 = jnp.float32
BF16 = jnp.bfloat16
PW = 896
QN = HALF * SEL
QPAD = 640
SCALE2 = math.log2(math.e) / math.sqrt(HD)
CHUNKS = [(0, 128), (128, 256), (384, 256), (640, 256)]
SLOT = {0: 0, 1: 1, 3: 2, 2: 3}
SEMS = 140


def spread(vec, lanes):
    return lax.dot_general(
        vec, jnp.ones((8, lanes), F32), (((0,), (0,)), ((), ())),
        precision=lax.Precision.HIGHEST, preferred_element_type=F32,
    )


def turned(v, c, sn):
    return v * c + pltpu.roll(v, 64, 1) * sn


def sublayer(owners, positions, rows, gain, freq, h_any, wq_any, wkv_any, store, wo_any,
             blended, mixed,
             h, wq, wkv, wo, st0, st1, stsend, strecv, p2, p2r, acc, psend, precv, zsend, zrecv,
             sqs, sqr, sqz, sqzr, trig, kvc, fr, keys, vt, first_kv, q, sbuf, pbuf, o, lse,
             orecv, lrecv, ag, prod, crecv, csum, xrecv, zlsend, zlrecv, ssem, rsem, lsem):
    s = lax.axis_index("section")
    t = lax.axis_index("tensor")
    y, z = s // 4, s % 4
    x, zl, core = t // 4, (t // 2) % 2, t % 2
    kind = t // 8
    values = kind == 1

    def ypeer(d):
        return {"section": ((y + d) % 4) * 4 + z}

    def zpeer(d):
        return {"section": y * 4 + (z + d) % 4}

    def xpeer(d):
        return {"tensor": ((x + d) % 4) * 4 + t % 4}

    twin = {"tensor": x * 4 + zl * 2 + 1 - core}
    pair = {"tensor": x * 4 + (1 - zl) * 2 + core}
    partner = xpeer(2)
    sent = []
    ids = [0]

    def push(src, dst, dev):
        i = ids[0]
        ids[0] += 1
        c = pltpu.make_async_remote_copy(
            src_ref=src, dst_ref=dst, send_sem=ssem.at[i], recv_sem=rsem.at[i],
            device_id=dev, device_id_type=MESH)
        c.start()
        sent.append(c)
        return c

    def waits(copies):
        for c in copies:
            c.wait_recv()

    st = [st0, st1]
    local = []

    def fetch(src, dst):
        c = pltpu.make_async_copy(src, dst, lsem.at[len(local)])
        c.start()
        local.append(c)

    fetch(h_any, h)
    fetch(wq_any, wq)
    fetch(wkv_any, wkv)
    fetch(store.at[:, pl.ds(0, LH)], st0.at[y])
    fetch(store.at[:, pl.ds(LH, LH)], st1.at[y])
    fetch(wo_any, wo)

    peers = [f(d) for f in (ypeer, zpeer, xpeer) for d in (1, 2, 3)] + [twin, pair]
    barrier = pltpu.get_barrier_semaphore()
    for peer in peers:
        pl.semaphore_signal(barrier, inc=1, device_id=peer, device_id_type=MESH)
    pl.semaphore_wait(barrier, len(peers))

    def send_store(k):
        src = store.at[:, pl.ds(k * LH, LH)]
        return [push(src, st[k].at[y], ypeer(1)), push(src, st[k].at[y], ypeer(3))]

    def forward_store(k, copies):
        waits(copies)
        below, above = (y + 3) % 4, (y + 1) % 4
        a, b = st[k].at[below, pl.ds(0, 2)], st[k].at[above, pl.ds(2, 2)]
        return [push(a, a, ypeer(1)), push(b, b, ypeer(3))]

    def picked(k, d):
        slot = owners[y * 4 + (z + d) % 4]
        here = ((slot >> 2) & 3) == z
        block = st[k][slot >> 4, slot & 3]
        return jnp.where(here, block, jnp.zeros_like(block))

    def route_store(k, copies):
        waits(copies)
        out = []
        for d in (1, 3, 2):
            stsend[k, d] = picked(k, d)
            out.append(push(stsend.at[k, d], strecv.at[k, 4 - d], zpeer(d)))
        return out

    ones8 = jnp.ones((8, 128), F32)
    gains = gain[...].astype(F32).reshape(1, 768)

    def multiply(d, out, i):
        hf = h[pl.ds(((y + d) % 4) * 4, 4)].astype(F32).reshape(4 * SEL, 768)
        hg = (hf * gains).astype(BF16)
        a = jnp.dot(hg, wkv[...], preferred_element_type=F32)
        b = jnp.dot(hg, wq[...], preferred_element_type=F32)
        out[i, :, :, :HD] = a.reshape(4, SEL, HD).astype(out.dtype)
        out[i, :, :, HD:] = b.reshape(4, SEL, 768).astype(out.dtype)
        sq = hf * hf
        part = sq[:, :128]
        for k in range(1, 6):
            part = part + sq[:, k * 128:(k + 1) * 128]
        sqs[d] = jnp.zeros((8, 128), F32)
        for g in range(4):
            row = lax.dot_general(
                ones8, part[g * SEL:(g + 1) * SEL], (((1,), (1,)), ((), ())),
                precision=lax.Precision.HIGHEST, preferred_element_type=F32)
            sqs[d, g:g + 1, :SEL] = row[:1]

    st_a = send_store(0)
    for c in local[:3]:
        c.wait()
    multiply(2, p2, 0)
    sq_y = [push(sqs.at[2], sqr.at[2], ypeer(2))]
    fw_a = forward_store(0, st_a)
    st_b = send_store(1)
    up2, dn2 = [], []
    for lo, n in CHUNKS:
        cols = pl.ds(lo, n)
        up2.append(push(p2.at[0, pl.ds(0, 2), :, cols], p2r.at[0, :, :, cols], ypeer(1)))
        dn2.append(push(p2.at[0, pl.ds(2, 2), :, cols], p2r.at[1, :, :, cols], ypeer(3)))
    multiply(1, acc, 1)
    sq_y.append(push(sqs.at[1], sqr.at[3], ypeer(1)))
    multiply(3, acc, 2)
    sq_y.append(push(sqs.at[3], sqr.at[1], ypeer(3)))
    local[3].wait()
    rt_a = route_store(0, fw_a)
    multiply(0, acc, 0)

    row8 = lax.broadcasted_iota(jnp.int32, (8, SEL), 0) == 0
    start = positions[s].astype(F32)
    my_rows = rows[pl.ds(s, 1), :].astype(F32)
    angle = spread(jnp.where(row8, my_rows + start, 0.0), HD) * freq[...]
    lane_sign = jnp.where(lax.broadcasted_iota(jnp.int32, (1, HD), 1) < 64, -1.0, 1.0)
    trig[0, :SEL] = jnp.cos(angle)
    trig[1, :SEL] = jnp.sin(angle) * lane_sign
    shift = jnp.broadcast_to(freq[...] * start, (8, HD))
    trig[0, SEL:] = jnp.where(values, 1.0, jnp.cos(shift))
    trig[1, SEL:] = jnp.where(values, 0.0, jnp.sin(shift) * lane_sign)
    q[:, QN:] = jnp.zeros((4, QPAD - QN, HD), BF16)
    tiled = (lax.broadcasted_iota(jnp.int32, (SEL, QPAD), 1) % SEL
             == lax.broadcasted_iota(jnp.int32, (SEL, QPAD), 0))
    limit = lax.dot_general(
        jnp.where(row8, my_rows, 0.0), jnp.where(tiled, 1.0, 0.0), (((1,), (0,)), ((), ())),
        precision=lax.Precision.HIGHEST, preferred_element_type=F32)[:1]

    fw_b = forward_store(1, st_b)
    up1, dn1 = [], []

    def send_near(k):
        lo, n = CHUNKS[k]
        cols = pl.ds(lo, n)
        up2[k].wait_recv()
        psend[0, :2, :, cols] = (acc[1, :2, :, cols] + p2r[0, :, :, cols].astype(F32)).astype(BF16)
        psend[0, 2:, :, cols] = acc[1, 2:, :, cols].astype(BF16)
        up1.append(push(psend.at[0, :, :, cols], precv.at[0, :, :, cols], ypeer(1)))
        dn2[k].wait_recv()
        psend[1, 2:, :, cols] = (acc[2, 2:, :, cols] + p2r[1, :, :, cols].astype(F32)).astype(BF16)
        psend[1, :2, :, cols] = acc[2, :2, :, cols].astype(BF16)
        dn1.append(push(psend.at[1, :, :, cols], precv.at[1, :, :, cols], ypeer(3)))

    send_near(0)
    waits(sq_y)
    sqz[...] = sqs[0] + sqr[1] + sqr[2] + sqr[3]
    sq_z = [push(sqz, sqzr.at[4 - d], zpeer(d)) for d in (1, 3, 2)]
    send_near(1)

    def settle(k, copies):
        cached = picked(k, 0)
        waits(copies)
        for d in (1, 2, 3):
            cached = cached + strecv[k, d]
        part = pl.ds(k * LH, LH)
        kvc[kind, 0, part] = turned(
            cached.astype(F32), trig[0, SEL:SEL + 1], trig[1, SEL:SEL + 1]).astype(BF16)
        mine = kvc.at[kind, 0, part]
        out = {4 - d: push(mine, kvc.at[kind, 4 - d, part], zpeer(d)) for d in (1, 3, 2)}
        return out, [push(mine, mine, partner)]

    kz_a, kx_a = settle(0, rt_a)
    local[4].wait()
    rt_b = route_store(1, fw_b)
    send_near(2)
    send_near(3)

    total = acc.at[0]
    pz = []

    def send_z(k):
        lo, n = CHUNKS[k]
        cols = pl.ds(lo, n)
        up1[k].wait_recv()
        dn1[k].wait_recv()
        out = []
        for d in (1, 3, 2):
            g = (z + d) % 4
            zsend[d, :, cols] = (total[g, :, cols] + precv[0, g, :, cols].astype(F32)
                                 + precv[1, g, :, cols].astype(F32)).astype(BF16)
            out.append(push(zsend.at[d, :, cols], zrecv.at[4 - d, :, cols], zpeer(d)))
        pz.append(out)

    def hand_over(k, kz, kx):
        part = pl.ds(k * LH, LH)
        for r in (3, 1, 2):
            kz[r].wait_recv()
            kx.append(push(kvc.at[kind, r, part], kvc.at[kind, r, part], partner))

    kz_b, kx_b = settle(1, rt_b)
    send_z(0)
    hand_over(0, kz_a, kx_a)
    send_z(1)

    waits(sq_z)
    squares = sqz[...] + sqzr[1] + sqzr[2] + sqzr[3]
    own = lax.broadcasted_iota(jnp.int32, (8, 128), 0) == z
    inv = lax.rsqrt(spread(jnp.where(own, squares, 0.0), HD)[:SEL] / D + EPS)

    def summed(lo):
        cols = pl.ds(lo, HD)
        v = (total[z, :, cols] + precv[0, z, :, cols].astype(F32)
             + precv[1, z, :, cols].astype(F32))
        for d in (1, 2, 3):
            v = v + zrecv[d, :, cols].astype(F32)
        return v * inv

    waits(pz[0])
    fr[kind, 0, :SEL] = turned(
        summed(0), jnp.where(values, 1.0, trig[0, :SEL]),
        jnp.where(values, 0.0, trig[1, :SEL])).astype(BF16)
    top_rows = pl.ds(0, SEL)
    fz = {4 - d: push(fr.at[kind, 0, top_rows], fr.at[kind, 4 - d, top_rows], zpeer(d))
          for d in (1, 3, 2)}
    fx = [push(fr.at[kind, 0, top_rows], fr.at[kind, 0, top_rows], partner)]
    send_z(2)
    hand_over(1, kz_b, kx_b)
    send_z(3)
    qy = {1: [], 2: [], 3: []}
    for k in (1, 2, 3):
        waits(pz[k])
        for j in (2 * k - 2, 2 * k - 1):
            q[0, j * SEL:(j + 1) * SEL] = turned(
                summed(HD + j * HD), trig[0, :SEL], trig[1, :SEL]).astype(BF16)
        part = pl.ds((k - 1) * 2 * SEL, 2 * SEL)
        for d in (1, 3, 2):
            qy[d].append(push(q.at[0, part], q.at[SLOT[4 - d], part], ypeer(d)))
        if k == 1:
            for r in (3, 1, 2):
                fz[r].wait_recv()
                fx.append(push(fr.at[kind, r, top_rows], fr.at[kind, r, top_rows], partner))

    waits(kx_a)
    waits(kx_b)
    waits(fx)
    for r in range(4):
        group = rows[pl.ds(y * 4 + (z + r) % 4, 1), :]
        hit = lax.broadcasted_iota(jnp.int32, (L, SEL), 0) == group
        hot = jnp.where(hit, 1.0, 0.0)
        taken = jnp.max(hot, axis=1, keepdims=True) > 0.0
        hot = hot.astype(BF16)
        for k in (0, 1):
            placed = jnp.dot(hot, fr[k, r, :SEL], preferred_element_type=F32)
            patched = jnp.where(taken, placed, kvc[k, r].astype(F32))
            if r == 0:
                first_kv[k] = patched.astype(BF16)
            if k == 0:
                keys[r] = patched.astype(BF16)
            else:
                vt[:, r * L:(r + 1) * L] = patched.T.astype(BF16)
    blended[...] = first_kv[kind]

    def attend(i, da, db):
        lane = lax.broadcasted_iota(jnp.int32, (1, 2 * QPAD), 1)
        at = jnp.where(lane < QPAD, positions[((y + da) % 4) * 4 + z],
                       positions[((y + db) % 4) * 4 + z])
        block = q[2 * i:2 * i + 2].reshape(2 * QPAD, HD)
        top = jnp.full((1, 2 * QPAD), MASKED, F32)
        hidden = []
        for e in range(4):
            sc = lax.dot_general(
                keys[e], block, (((1,), (1,)), ((), ())), preferred_element_type=F32)
            if i == 0 and e == 0:
                line = lax.broadcasted_iota(jnp.int32, (L, QPAD), 0).astype(F32)
                sc = jnp.concatenate(
                    [jnp.where(line <= limit, sc[:, :QPAD], MASKED), sc[:, QPAD:]], axis=1)
            sbuf[e] = sc
            hid = positions[y * 4 + (z + e) % 4] > at
            hidden.append(hid)
            top = jnp.maximum(top, jnp.where(hid, MASKED, jnp.max(sc, axis=0, keepdims=True)))
        top = top * SCALE2
        weight = jnp.zeros((1, 2 * QPAD), F32)
        for e in range(4):
            base = top + jnp.where(hidden[e], 1e30, 0.0)
            p = jnp.exp2(sbuf[e] * SCALE2 - base)
            weight = weight + jnp.sum(p, axis=0, keepdims=True)
            pbuf[e] = p.astype(BF16)
        num = jnp.dot(vt[...], pbuf[...].reshape(4 * L, 2 * QPAD), preferred_element_type=F32)
        some = weight > 0.0
        safe = jnp.where(some, weight, 1.0)
        o[2 * i:2 * i + 2] = (num * (1.0 / safe)).T.astype(BF16).reshape(2, QPAD, HD)
        logs = jnp.broadcast_to(jnp.where(some, top + jnp.log2(safe), MASKED), (8, 2 * QPAD))
        lse[2 * i] = logs[:, :QPAD]
        lse[2 * i + 1] = logs[:, QPAD:]

    got = {}

    def send_part(d):
        got[4 - d] = [push(o.at[SLOT[d], pl.ds(0, QN)], orecv.at[4 - d], ypeer(d)),
                      push(lse.at[SLOT[d]], lrecv.at[4 - d], ypeer(d))]

    waits(qy[3])
    attend(0, 0, 1)
    send_part(1)
    waits(qy[1])
    waits(qy[2])
    attend(1, 3, 2)
    send_part(2)
    send_part(3)

    for r in (3, 2, 1):
        waits(got[r])
    logs = [lse[0, :1]] + [lrecv[r, :1] for r in (1, 2, 3)]
    top = jnp.maximum(jnp.maximum(logs[0], logs[1]), jnp.maximum(logs[2], logs[3]))
    share = [jnp.exp2(v - top) for v in logs]
    whole = share[0] + share[1] + share[2] + share[3]
    line = lax.broadcasted_iota(jnp.int32, (8, QPAD), 0) == 0
    merged = jnp.zeros((QN, HD), F32)
    for r in range(4):
        part = o[0, :QN] if r == 0 else orecv[r]
        col = spread(jnp.where(line, share[r] / whole, 0.0), HD)[:QN]
        merged = merged + part.astype(F32) * col
    for j in range(HALF):
        ag[0, z, :, j * HD:(j + 1) * HD] = merged[j * SEL:(j + 1) * SEL].astype(BF16)

    def grp(d):
        return (z + d) % 4

    ups, dns = {}, {}

    def send_y(d):
        ups[d] = push(ag.at[0, grp(d)], ag.at[3, grp(d)], ypeer(1))
        dns[d] = push(ag.at[0, grp(d)], ag.at[1, grp(d)], ypeer(3))

    zs = {d: push(ag.at[0, z], ag.at[0, z], zpeer(d)) for d in (1, 3)}
    send_y(0)
    zs[2] = push(ag.at[0, z], ag.at[0, z], zpeer(2))
    for d in (3, 1, 2):
        zs[4 - d].wait_recv()
        send_y(d)
    local[5].wait()

    def multiply_out(r):
        a = jnp.dot(ag[r].reshape(4 * SEL, 768), wo[...], preferred_element_type=F32)
        a = a.reshape(4, SEL, 768).astype(BF16)
        for g in range(4):
            prod[r, g % 2, g // 2] = a[g]
        return push(prod.at[r, 1 - core], crecv.at[r], twin)

    xbase = 130

    def x_copy(r, slot):
        return pltpu.make_async_remote_copy(
            src_ref=csum.at[r], dst_ref=xrecv.at[slot], send_sem=ssem.at[xbase + r],
            recv_sem=rsem.at[xbase + slot], device_id=xpeer(4 - slot), device_id_type=MESH)

    def away(r):
        return (y + r + 4 - x) % 4

    def send_x(r, c):
        c.wait_recv()
        csum[r] = (prod[r, core].astype(F32) + crecv[r].astype(F32)).astype(BF16)

        @pl.when(away(r) != 0)
        def _():
            x_copy(r, (4 - away(r)) % 4).start()

    tw0 = multiply_out(0)
    fw = {}
    for d in (0, 3, 1, 2):
        ups[d].wait_recv()
        dns[d].wait_recv()
        if d in (0, 3):
            fw[d] = push(ag.at[3, grp(d)], ag.at[2, grp(d)], ypeer(1))
        else:
            fw[d] = push(ag.at[1, grp(d)], ag.at[2, grp(d)], ypeer(3))
    send_x(0, tw0)
    tw1 = multiply_out(1)
    tw3 = multiply_out(3)
    send_x(1, tw1)
    send_x(3, tw3)
    for d in (0, 3, 1, 2):
        fw[d].wait_recv()
    tw2 = multiply_out(2)
    send_x(2, tw2)

    for slot in (1, 2, 3):
        x_copy(0, slot).wait_recv()
    home = (x + 4 - y) % 4

    def reduced(k):
        v = csum[home, k].astype(F32)
        for slot in (1, 2, 3):
            v = v + xrecv[slot, k].astype(F32)
        return v

    zlsend[...] = reduced(1 - zl).astype(BF16)
    last = push(zlsend, zlrecv, pair)
    keep = reduced(zl)
    last.wait_recv()
    mixed[...] = (keep + zlrecv[...].astype(F32)).astype(BF16)
    for r in range(4):
        @pl.when(away(r) != 0)
        def _():
            x_copy(r, 1).wait_send()
    for c in sent:
        c.wait_send()
    assert ids[0] <= xbase


VM = pl.BlockSpec(memory_space=pltpu.VMEM)
SM = pl.BlockSpec(memory_space=pltpu.SMEM)
ANY = pl.BlockSpec(memory_space=pl.ANY)
FREQ = (THETA ** (-2.0 * (np.arange(HD) % (HD // 2)) / HD)).astype(np.float32)[None]


def shards(store, owners, positions, sel_rows, sel_hidden, norm_gain, w_query, w_keyval, w_out):
    blended, mixed = pl.pallas_call(
        sublayer,
        name="sublayer",
        out_shape=(
            jax.ShapeDtypeStruct((L, HD), BF16),
            jax.ShapeDtypeStruct((SEL, 768), BF16),
        ),
        in_specs=[SM, SM, VM, VM, VM, ANY, ANY, ANY, ANY, ANY],
        out_specs=(VM, VM),
        scratch_shapes=[
            pltpu.VMEM((16, SEL, 768), BF16),
            pltpu.VMEM((768, 768), BF16),
            pltpu.VMEM((768, HD), BF16),
            pltpu.VMEM((768, 768), BF16),
            pltpu.VMEM((4, 4, LH, HD), BF16),
            pltpu.VMEM((4, 4, LH, HD), BF16),
            pltpu.VMEM((2, 4, LH, HD), BF16),
            pltpu.VMEM((2, 4, LH, HD), BF16),
            pltpu.VMEM((1, 4, SEL, PW), BF16),
            pltpu.VMEM((2, 2, SEL, PW), BF16),
            pltpu.VMEM((3, 4, SEL, PW), F32),
            pltpu.VMEM((2, 4, SEL, PW), BF16),
            pltpu.VMEM((2, 4, SEL, PW), BF16),
            pltpu.VMEM((4, SEL, PW), BF16),
            pltpu.VMEM((4, SEL, PW), BF16),
            pltpu.VMEM((4, 8, 128), F32),
            pltpu.VMEM((4, 8, 128), F32),
            pltpu.VMEM((8, 128), F32),
            pltpu.VMEM((4, 8, 128), F32),
            pltpu.VMEM((2, SEL + 8, HD), F32),
            pltpu.VMEM((2, 4, L, HD), BF16),
            pltpu.VMEM((2, 4, SEL, HD), BF16),
            pltpu.VMEM((4, L, HD), BF16),
            pltpu.VMEM((HD, 4 * L), BF16),
            pltpu.VMEM((2, L, HD), BF16),
            pltpu.VMEM((4, QPAD, HD), BF16),
            pltpu.VMEM((4, L, 2 * QPAD), F32),
            pltpu.VMEM((4, L, 2 * QPAD), BF16),
            pltpu.VMEM((4, QPAD, HD), BF16),
            pltpu.VMEM((4, 8, QPAD), F32),
            pltpu.VMEM((4, QN, HD), BF16),
            pltpu.VMEM((4, 8, QPAD), F32),
            pltpu.VMEM((4, 4, SEL, 768), BF16),
            pltpu.VMEM((4, 2, 2, SEL, 768), BF16),
            pltpu.VMEM((4, 2, SEL, 768), BF16),
            pltpu.VMEM((4, 2, SEL, 768), BF16),
            pltpu.VMEM((4, 2, SEL, 768), BF16),
            pltpu.VMEM((SEL, 768), BF16),
            pltpu.VMEM((SEL, 768), BF16),
            pltpu.SemaphoreType.DMA((SEMS,)),
            pltpu.SemaphoreType.DMA((SEMS,)),
            pltpu.SemaphoreType.DMA((6,)),
        ],
        compiler_params=pltpu.CompilerParams(
            collective_id=0, has_side_effects=True, vmem_limit_bytes=60 * 2**20),
    )(owners, positions, sel_rows, norm_gain, jnp.asarray(FREQ),
      sel_hidden, w_query, w_keyval, store, w_out)
    return blended[None], mixed[None]


def solution(mesh):
    return jax.shard_map(
        shards,
        mesh=mesh,
        in_specs=(
            P("section", None, "tensor"),
            P(),
            P(),
            P(),
            P(None, None, "section"),
            P("section"),
            P("section", "tensor"),
            P("section", "tensor"),
            P("tensor", "section"),
        ),
        out_specs=(P("section", None, "tensor"), P("tensor", None, "section")),
        check_vma=False,
    )
```

time: 690 us -> 161 us (0.23)
  the two profiles are of different devices: /device:TPU:36 before, /device:TPU:90 now
where the time goes in v2:
time: 161 us
  Pallas kernels  157 us (98%)
  local copies, waits for them, and re-layouts  3.17 us (2%)
    pallas_call x1, Pallas kernels, shards(): pl.pallas_call(sublayer, name='sublayer', out_shape=(jax.ShapeDtypeStruct...  157 us

profile of v2, /device:TPU:90, one launch (start us, length us, event | category | flops | bytes accessed | tf_op | source)
XLA Modules:
  0.0 161.2 jit_solution(18329260416861959871)
XLA Ops:
  0.6 157.4 %sublayer.1 = (bf16[640,128]{1,0:T(8,128)(2,1)}, bf16[96,768]{1,0:T(8,128)(2,1)}) custom-call(s32[16]{0:T(128)} %owners.1, s32[16]{0:T(128)} %positions.1, s32[16,96]{1,0:T(8,128)} %rows.1, bf16[768]{0:T(1024)(128)(2,1)} %gain.1, f32[1,128]{1,0:T(1,128)} %constant.2.clone.freq, bf16[16,96,768]{2,1,0:T(8,128)(2,1)} %h_any.1, bf16[768,768]{1,0:T(8,128)(2,1)} %wq_any.1, ...), custom_call_target="tpu_custom_call" | custom-call | tf_op jit(solution)/shard_map/sublayer/pallas_call | solution.py:466
  158.0 1.6 copy.14
  159.6 1.6 copy.15

commit v3 on v2

v3 whole, which is shorter than its diff:
```python
import math

import jax
import jax.numpy as jnp
import numpy as np
from jax import lax
from jax.experimental import pallas as pl
from jax.experimental.pallas import tpu as pltpu
from jax.sharding import PartitionSpec as P

D = 12288
HD = 128
HALF = 6
L = 640
SEL = 96
THETA = 1000000.0
EPS = 1e-05
MASKED = -1e30
MESH = pl.DeviceIdType.MESH
F32 = jnp.float32
BF16 = jnp.bfloat16
PW = 896
QN = HALF * SEL
QC = 2 * SEL
TQ = 4 * QC
PARTS = [(0, 128), (128, 256), (384, 256)]
NP = len(PARTS)
OC = 384
SCALE2 = math.log2(math.e) / math.sqrt(HD)
CHUNKS = [(0, 128), (128, 256), (384, 256), (640, 256)]
XBASE = 180
SEMS = 200


def spread(vec, lanes):
    return lax.dot_general(
        vec, jnp.ones((8, lanes), F32), (((0,), (0,)), ((), ())),
        precision=lax.Precision.HIGHEST, preferred_element_type=F32,
    )


def turned(v, c, sn):
    return v * c + pltpu.roll(v, 64, 1) * sn


def sublayer(owners, positions, rows, gain, freq, h_any, wq_any, wkv_any, store, wo_any,
             blended, mixed,
             h, wq, wkv, wo, st0, st1, st2, stsend, strecv, p2, p2r, acc, psend, precv, zsend,
             zrecv, sqs, sqr, sqz, sqzr, trig, kvc, fr, keys, vt, first_kv, q, sbuf, pbuf, o, lse,
             orecv, lrecv, ag, prod, crecv, csum, zlrecv, xsum, xrecv, ssem, rsem, lsem):
    s = lax.axis_index("section")
    t = lax.axis_index("tensor")
    y, z = s // 4, s % 4
    x, zl, core = t // 4, (t // 2) % 2, t % 2
    kind = t // 8
    values = kind == 1

    def ypeer(d):
        return {"section": ((y + d) % 4) * 4 + z}

    def zpeer(d):
        return {"section": y * 4 + (z + d) % 4}

    def xpeer(d):
        return {"tensor": ((x + d) % 4) * 4 + t % 4}

    twin = {"tensor": x * 4 + zl * 2 + 1 - core}
    pair = {"tensor": x * 4 + (1 - zl) * 2 + core}
    partner = xpeer(2)
    sent = []
    ids = [0]

    def push(src, dst, dev):
        i = ids[0]
        ids[0] += 1
        c = pltpu.make_async_remote_copy(
            src_ref=src, dst_ref=dst, send_sem=ssem.at[i], recv_sem=rsem.at[i],
            device_id=dev, device_id_type=MESH)
        c.start()
        sent.append(c)
        return c

    def waits(copies):
        for c in copies:
            c.wait_recv()

    st = [st0, st1, st2]
    local = []

    def fetch(src, dst):
        c = pltpu.make_async_copy(src, dst, lsem.at[len(local)])
        c.start()
        local.append(c)

    fetch(h_any, h)
    fetch(wq_any, wq)
    fetch(wkv_any, wkv)
    for k, (lo, n) in enumerate(PARTS):
        fetch(store.at[:, pl.ds(lo, n)], st[k].at[y])
    fetch(wo_any, wo)

    peers = [f(d) for f in (ypeer, zpeer, xpeer) for d in (1, 2, 3)] + [twin, pair]
    barrier = pltpu.get_barrier_semaphore()
    for peer in peers:
        pl.semaphore_signal(barrier, inc=1, device_id=peer, device_id_type=MESH)
    pl.semaphore_wait(barrier, len(peers))

    def send_store(k):
        src = store.at[:, pl.ds(*PARTS[k])]
        return [push(src, st[k].at[y], ypeer(1)), push(src, st[k].at[y], ypeer(3))]

    def forward_store(k, copies):
        waits(copies)
        below, above = (y + 3) % 4, (y + 1) % 4
        a, b = st[k].at[below, pl.ds(0, 2)], st[k].at[above, pl.ds(2, 2)]
        return [push(a, a, ypeer(1)), push(b, b, ypeer(3))]

    def picked(k, d):
        slot = owners[y * 4 + (z + d) % 4]
        here = ((slot >> 2) & 3) == z
        block = st[k][slot >> 4, slot & 3]
        return jnp.where(here, block, jnp.zeros_like(block))

    def route_store(k, copies):
        local[3 + k].wait()
        waits(copies)
        part = pl.ds(*PARTS[k])
        out = []
        for d in (1, 3, 2):
            stsend[d, part] = picked(k, d)
            out.append(push(stsend.at[d, part], strecv.at[4 - d, part], zpeer(d)))
        return out

    ones8 = jnp.ones((8, 128), F32)
    gains = gain[...].astype(F32).reshape(1, 768)

    def multiply(d, out, i):
        hf = h[pl.ds(((y + d) % 4) * 4, 4)].astype(F32).reshape(4 * SEL, 768)
        hg = (hf * gains).astype(BF16)
        a = jnp.dot(hg, wkv[...], preferred_element_type=F32)
        b = jnp.dot(hg, wq[...], preferred_element_type=F32)
        out[i, :, :, :HD] = a.reshape(4, SEL, HD).astype(out.dtype)
        out[i, :, :, HD:] = b.reshape(4, SEL, 768).astype(out.dtype)
        sq = hf * hf
        part = sq[:, :128]
        for k in range(1, 6):
            part = part + sq[:, k * 128:(k + 1) * 128]
        sqs[d] = jnp.zeros((8, 128), F32)
        for g in range(4):
            row = lax.dot_general(
                ones8, part[g * SEL:(g + 1) * SEL], (((1,), (1,)), ((), ())),
                precision=lax.Precision.HIGHEST, preferred_element_type=F32)
            sqs[d, g:g + 1, :SEL] = row[:1]

    up2, dn2, up1, dn1 = [], [], [], []

    def send_far(k):
        cols = pl.ds(*CHUNKS[k])
        up2.append(push(p2.at[0, pl.ds(0, 2), :, cols], p2r.at[0, :, :, cols], ypeer(1)))
        dn2.append(push(p2.at[0, pl.ds(2, 2), :, cols], p2r.at[1, :, :, cols], ypeer(3)))

    def send_near(k):
        cols = pl.ds(*CHUNKS[k])
        up2[k].wait_recv()
        psend[0, :2, :, cols] = (acc[1, :2, :, cols] + p2r[0, :, :, cols].astype(F32)).astype(BF16)
        psend[0, 2:, :, cols] = acc[1, 2:, :, cols].astype(BF16)
        up1.append(push(psend.at[0, :, :, cols], precv.at[0, :, :, cols], ypeer(1)))
        dn2[k].wait_recv()
        psend[1, 2:, :, cols] = (acc[2, 2:, :, cols] + p2r[1, :, :, cols].astype(F32)).astype(BF16)
        psend[1, :2, :, cols] = acc[2, :2, :, cols].astype(BF16)
        dn1.append(push(psend.at[1, :, :, cols], precv.at[1, :, :, cols], ypeer(3)))

    total = acc.at[0]

    def send_z(k):
        cols = pl.ds(*CHUNKS[k])
        up1[k].wait_recv()
        dn1[k].wait_recv()
        out = []
        for d in (1, 3, 2):
            g = (z + d) % 4
            zsend[d, :, cols] = (total[g, :, cols] + precv[0, g, :, cols].astype(F32)
                                 + precv[1, g, :, cols].astype(F32)).astype(BF16)
            out.append(push(zsend.at[d, :, cols], zrecv.at[4 - d, :, cols], zpeer(d)))
        return out

    def settle(k, copies):
        cached = picked(k, 0)
        waits(copies)
        part = pl.ds(*PARTS[k])
        for d in (1, 2, 3):
            cached = cached + strecv[d, part]
        kvc[kind, 0, part] = turned(
            cached.astype(F32), trig[0, SEL:SEL + 1], trig[1, SEL:SEL + 1]).astype(BF16)
        mine = kvc.at[kind, 0, part]
        out = {4 - d: push(mine, kvc.at[kind, 4 - d, part], zpeer(d)) for d in (1, 3)}
        return out, [push(mine, mine, partner)]

    def pass_on(k, kz, kx):
        lo, n = PARTS[k]
        part = pl.ds(lo, n)
        for r, half, to in ((1, lo, 3), (3, lo + n // 2, 1)):
            kz[r].wait_recv()
            half = pl.ds(half, n // 2)
            kz[r + 4] = push(kvc.at[kind, r, half], kvc.at[kind, 2, half], zpeer(to))
            kx.append(push(kvc.at[kind, r, part], kvc.at[kind, r, part], partner))

    def pass_far(k, kz, kx):
        part = pl.ds(*PARTS[k])
        kz[5].wait_recv()
        kz[7].wait_recv()
        kx.append(push(kvc.at[kind, 2, part], kvc.at[kind, 2, part], partner))

    sa = send_store(0)
    for c in local[:3]:
        c.wait()
    multiply(2, p2, 0)
    sb = send_store(1)
    sq_y = [push(sqs.at[2], sqr.at[2], ypeer(2))]
    fa = forward_store(0, sa)
    send_far(0)
    send_far(1)
    multiply(1, acc, 1)
    sq_y.append(push(sqs.at[1], sqr.at[3], ypeer(1)))
    ra = route_store(0, fa)
    multiply(3, acc, 2)
    sq_y.append(push(sqs.at[3], sqr.at[1], ypeer(3)))
    sc = send_store(2)
    fb = forward_store(1, sb)

    row8 = lax.broadcasted_iota(jnp.int32, (8, SEL), 0) == 0
    start = positions[s].astype(F32)
    my_rows = rows[pl.ds(s, 1), :].astype(F32)
    angle = spread(jnp.where(row8, my_rows + start, 0.0), HD) * freq[...]
    lane_sign = jnp.where(lax.broadcasted_iota(jnp.int32, (1, HD), 1) < 64, -1.0, 1.0)
    trig[0, :SEL] = jnp.cos(angle)
    trig[1, :SEL] = jnp.sin(angle) * lane_sign
    shift = jnp.broadcast_to(freq[...] * start, (8, HD))
    trig[0, SEL:] = jnp.where(values, 1.0, jnp.cos(shift))
    trig[1, SEL:] = jnp.where(values, 0.0, jnp.sin(shift) * lane_sign)
    kz_a, kx_a = settle(0, ra)
    multiply(0, acc, 0)
    send_far(2)
    send_far(3)
    send_near(0)
    send_near(1)
    waits(sq_y)
    sqz[...] = sqs[0] + sqr[1] + sqr[2] + sqr[3]
    sq_z = [push(sqz, sqzr.at[4 - d], zpeer(d)) for d in (1, 3, 2)]
    rb = route_store(1, fb)
    pass_on(0, kz_a, kx_a)
    fc = forward_store(2, sc)
    kz_b, kx_b = settle(1, rb)
    send_near(2)
    pass_far(0, kz_a, kx_a)
    pz = [send_z(0)]
    rc = route_store(2, fc)
    send_near(3)
    pass_on(1, kz_b, kx_b)
    pz.append(send_z(1))
    kz_c, kx_c = settle(2, rc)
    pass_far(1, kz_b, kx_b)

    waits(sq_z)
    squares = sqz[...] + sqzr[1] + sqzr[2] + sqzr[3]
    own = lax.broadcasted_iota(jnp.int32, (8, 128), 0) == z
    inv = lax.rsqrt(spread(jnp.where(own, squares, 0.0), HD)[:SEL] / D + EPS)

    def summed(lo):
        cols = pl.ds(lo, HD)
        v = (total[z, :, cols] + precv[0, z, :, cols].astype(F32)
             + precv[1, z, :, cols].astype(F32))
        for d in (1, 2, 3):
            v = v + zrecv[d, :, cols].astype(F32)
        return v * inv

    waits(pz[0])
    fr[kind, 0] = turned(
        summed(0), jnp.where(values, 1.0, trig[0, :SEL]),
        jnp.where(values, 0.0, trig[1, :SEL])).astype(BF16)
    fz = {4 - d: push(fr.at[kind, 0], fr.at[kind, 4 - d], zpeer(d)) for d in (1, 3, 2)}
    fx = [push(fr.at[kind, 0], fr.at[kind, 0], partner)]
    pass_on(2, kz_c, kx_c)
    pz.append(send_z(2))
    qy = []

    def send_queries(k):
        waits(pz[k + 1])
        for j in (0, 1):
            q[k, j * SEL:(j + 1) * SEL] = turned(
                summed(HD + (2 * k + j) * HD), trig[0, :SEL], trig[1, :SEL]).astype(BF16)
        mine = q.at[k, pl.ds(0, QC)]
        qy.append([push(mine, q.at[k, pl.ds((4 - d) * QC, QC)], ypeer(d)) for d in (1, 3, 2)])

    send_queries(0)
    pass_far(2, kz_c, kx_c)
    for r in (3, 1, 2):
        fz[r].wait_recv()
        fx.append(push(fr.at[kind, r], fr.at[kind, r], partner))
    pz.append(send_z(3))
    send_queries(1)

    waits(kx_a)
    waits(kx_b)
    waits(kx_c)
    waits(fx)
    for r in range(4):
        group = rows[pl.ds(y * 4 + (z + r) % 4, 1), :]
        hit = lax.broadcasted_iota(jnp.int32, (L, SEL), 0) == group
        hot = jnp.where(hit, 1.0, 0.0)
        taken = jnp.max(hot, axis=1, keepdims=True) > 0.0
        hot = hot.astype(BF16)
        for k in (0, 1):
            placed = jnp.dot(hot, fr[k, r], preferred_element_type=F32)
            patched = jnp.where(taken, placed, kvc[k, r].astype(F32))
            if r == 0:
                first_kv[k] = patched.astype(BF16)
            if k == 0:
                keys[r] = patched.astype(BF16)
            else:
                vt[:, r * L:(r + 1) * L] = patched.T.astype(BF16)
    blended[...] = first_kv[kind]

    lane = lax.broadcasted_iota(jnp.int32, (1, TQ), 1)
    first = jnp.full((1, TQ), positions[y * 4 + z], jnp.int32)
    for d in (1, 2, 3):
        first = jnp.where(lane >= d * QC, positions[((y + d) % 4) * 4 + z], first)
    tiled = (lax.broadcasted_iota(jnp.int32, (SEL, TQ), 1) % SEL
             == lax.broadcasted_iota(jnp.int32, (SEL, TQ), 0))
    limit = lax.dot_general(
        jnp.where(row8, my_rows, 0.0), jnp.where(tiled, 1.0, 0.0), (((1,), (0,)), ((), ())),
        precision=lax.Precision.HIGHEST, preferred_element_type=F32)[:1]
    limit = jnp.where(lane < QC, limit, float(L))
    hidden = [positions[y * 4 + (z + e) % 4] > first for e in range(4)]

    def attend(k):
        waits(qy[k])
        block = q[k]
        top = jnp.full((1, TQ), MASKED, F32)
        for e in range(4):
            sc = lax.dot_general(
                keys[e], block, (((1,), (1,)), ((), ())), preferred_element_type=F32)
            if e == 0:
                line = lax.broadcasted_iota(jnp.int32, (L, TQ), 0).astype(F32)
                sc = jnp.where(line <= limit, sc, MASKED)
            sbuf[e] = sc
            top = jnp.maximum(
                top, jnp.where(hidden[e], MASKED, jnp.max(sc, axis=0, keepdims=True)))
        top = top * SCALE2
        weight = jnp.zeros((1, TQ), F32)
        for e in range(4):
            base = top + jnp.where(hidden[e], 1e30, 0.0)
            p = jnp.exp2(sbuf[e] * SCALE2 - base)
            weight = weight + jnp.sum(p, axis=0, keepdims=True)
            pbuf[e] = p.astype(BF16)
        num = jnp.dot(vt[...], pbuf[...].reshape(4 * L, TQ), preferred_element_type=F32)
        some = weight > 0.0
        safe = jnp.where(some, weight, 1.0)
        o[k] = (num * (1.0 / safe)).T.astype(BF16)
        logs = jnp.broadcast_to(jnp.where(some, top + jnp.log2(safe), MASKED), (8, TQ))
        for d in range(4):
            moved = pltpu.roll(logs, TQ - d * QC, 1) if d else logs
            lse[k, d] = moved[:, :256]
        got = {}
        for d in (2, 1, 3):
            got[4 - d] = [push(o.at[k, pl.ds(d * QC, QC)], orecv.at[k, 4 - d], ypeer(d)),
                          push(lse.at[k, d], lrecv.at[k, 4 - d], ypeer(d))]
        return got

    def merge(k, got):
        for r in (1, 3, 2):
            waits(got[r])
        logs = [lse[k, 0, :1]] + [lrecv[k, r, :1] for r in (1, 2, 3)]
        top = jnp.maximum(jnp.maximum(logs[0], logs[1]), jnp.maximum(logs[2], logs[3]))
        share = [jnp.exp2(v - top) for v in logs]
        whole = share[0] + share[1] + share[2] + share[3]
        line = lax.broadcasted_iota(jnp.int32, (8, 256), 0) == 0
        merged = jnp.zeros((QC, HD), F32)
        for r in range(4):
            part = o[k, :QC] if r == 0 else orecv[k, r]
            col = spread(jnp.where(line, share[r] / whole, 0.0), HD)[:QC]
            merged = merged + part.astype(F32) * col
        for j in (0, 1):
            lo = (2 * k + j) * HD
            ag[0, z, :, lo:lo + HD] = merged[j * SEL:(j + 1) * SEL].astype(BF16)

    zs, ups, dns, fw = {}, {}, {}, {}

    def block_of(r, k, d):
        return ag.at[r, (z + d) % 4, :, pl.ds(k * 256, 256)]

    def send_y(k, d):
        ups[k, d] = push(block_of(0, k, d), block_of(3, k, d), ypeer(1))
        dns[k, d] = push(block_of(0, k, d), block_of(1, k, d), ypeer(3))

    def gather_start(k, got):
        merge(k, got)
        mine = block_of(0, k, 0)
        zs[k, 1] = push(mine, mine, zpeer(1))
        zs[k, 3] = push(mine, mine, zpeer(3))
        send_y(k, 0)
        zs[k, 2] = push(mine, mine, zpeer(2))

    def gather_z(k):
        for d in (3, 1, 2):
            zs[k, 4 - d].wait_recv()
            send_y(k, d)

    def gather_far(k):
        for d in (0, 3, 1, 2):
            ups[k, d].wait_recv()
            dns[k, d].wait_recv()
            if d in (0, 3):
                fw[k, d] = push(block_of(3, k, d), block_of(2, k, d), ypeer(1))
            else:
                fw[k, d] = push(block_of(1, k, d), block_of(2, k, d), ypeer(3))

    def multiply_out(r, c):
        cols = pl.ds(c * OC, OC)
        a = jnp.dot(ag[r].reshape(4 * SEL, 768), wo[:, cols], preferred_element_type=F32)
        a = a.reshape(4, SEL, OC).astype(BF16)
        for g in range(4):
            prod[r, c, g % 2, g // 2] = a[g]
        return push(prod.at[r, c, 1 - core], crecv.at[r, c], twin)

    def send_zl(r, c, copy):
        copy.wait_recv()
        csum[r, c] = (prod[r, c, core].astype(F32) + crecv[r, c].astype(F32)).astype(BF16)
        return push(csum.at[r, c, 1 - zl], zlrecv.at[r, c], pair)

    def x_copy(r, c, slot):
        return pltpu.make_async_remote_copy(
            src_ref=xsum.at[r, c], dst_ref=xrecv.at[slot, c], send_sem=ssem.at[XBASE + 2 * r + c],
            recv_sem=rsem.at[XBASE + 2 * slot + c], device_id=xpeer(4 - slot),
            device_id_type=MESH)

    def away(r):
        return (y + r + 4 - x) % 4

    def send_x(r, c, copy):
        copy.wait_recv()
        xsum[r, c] = (csum[r, c, zl].astype(F32) + zlrecv[r, c].astype(F32)).astype(BF16)

        @pl.when(away(r) != 0)
        def _():
            x_copy(r, c, (4 - away(r)) % 4).start()

    g0 = attend(0)
    send_queries(2)
    g1 = attend(1)
    gather_start(0, g0)
    g2 = attend(2)
    gather_z(0)
    gather_start(1, g1)
    gather_z(1)
    gather_start(2, g2)
    gather_far(0)
    gather_z(2)
    gather_far(1)
    local[3 + NP].wait()
    tw = {(0, c): multiply_out(0, c) for c in (0, 1)}
    gather_far(2)
    zz = {}
    for r in (1, 3):
        for c in (0, 1):
            tw[r, c] = multiply_out(r, c)
    for r in (0, 1, 3):
        for c in (0, 1):
            zz[r, c] = send_zl(r, c, tw[r, c])
    for c in (0, 1):
        send_x(0, c, zz[0, c])
    for k in range(3):
        for d in (0, 3, 1, 2):
            fw[k, d].wait_recv()
    for c in (0, 1):
        tw[2, c] = multiply_out(2, c)
    for r in (1, 3):
        for c in (0, 1):
            send_x(r, c, zz[r, c])
    for c in (0, 1):
        zz[2, c] = send_zl(2, c, tw[2, c])
    for c in (0, 1):
        send_x(2, c, zz[2, c])
    home = (x + 4 - y) % 4
    for c in (0, 1):
        v = xsum[home, c].astype(F32)
        for slot in (1, 2, 3):
            x_copy(0, c, slot).wait_recv()
            v = v + xrecv[slot, c].astype(F32)
        mixed[:, c * OC:(c + 1) * OC] = v.astype(BF16)
    for r in range(4):
        @pl.when(away(r) != 0)
        def _():
            for c in (0, 1):
                x_copy(r, c, 1).wait_send()
    for c in sent:
        c.wait_send()
    assert ids[0] <= XBASE


VM = pl.BlockSpec(memory_space=pltpu.VMEM)
SM = pl.BlockSpec(memory_space=pltpu.SMEM)
ANY = pl.BlockSpec(memory_space=pl.ANY)
FREQ = (THETA ** (-2.0 * (np.arange(HD) % (HD // 2)) / HD)).astype(np.float32)[None]


def shards(store, owners, positions, sel_rows, sel_hidden, norm_gain, w_query, w_keyval, w_out):
    blended, mixed = pl.pallas_call(
        sublayer,
        name="sublayer",
        out_shape=(
            jax.ShapeDtypeStruct((L, HD), BF16),
            jax.ShapeDtypeStruct((SEL, 768), BF16),
        ),
        in_specs=[SM, SM, VM, VM, VM, ANY, ANY, ANY, ANY, ANY],
        out_specs=(VM, VM),
        scratch_shapes=[
            pltpu.VMEM((16, SEL, 768), BF16),
            pltpu.VMEM((768, 768), BF16),
            pltpu.VMEM((768, HD), BF16),
            pltpu.VMEM((768, 768), BF16),
            *[pltpu.VMEM((4, 4, n, HD), BF16) for _, n in PARTS],
            pltpu.VMEM((4, L, HD), BF16),
            pltpu.VMEM((4, L, HD), BF16),
            pltpu.VMEM((1, 4, SEL, PW), BF16),
            pltpu.VMEM((2, 2, SEL, PW), BF16),
            pltpu.VMEM((3, 4, SEL, PW), F32),
            pltpu.VMEM((2, 4, SEL, PW), BF16),
            pltpu.VMEM((2, 4, SEL, PW), BF16),
            pltpu.VMEM((4, SEL, PW), BF16),
            pltpu.VMEM((4, SEL, PW), BF16),
            pltpu.VMEM((4, 8, 128), F32),
            pltpu.VMEM((4, 8, 128), F32),
            pltpu.VMEM((8, 128), F32),
            pltpu.VMEM((4, 8, 128), F32),
            pltpu.VMEM((2, SEL + 8, HD), F32),
            pltpu.VMEM((2, 4, L, HD), BF16),
            pltpu.VMEM((2, 4, SEL, HD), BF16),
            pltpu.VMEM((4, L, HD), BF16),
            pltpu.VMEM((HD, 4 * L), BF16),
            pltpu.VMEM((2, L, HD), BF16),
            pltpu.VMEM((3, TQ, HD), BF16),
            pltpu.VMEM((4, L, TQ), F32),
            pltpu.VMEM((4, L, TQ), BF16),
            pltpu.VMEM((3, TQ, HD), BF16),
            pltpu.VMEM((3, 4, 8, 256), F32),
            pltpu.VMEM((3, 4, QC, HD), BF16),
            pltpu.VMEM((3, 4, 8, 256), F32),
            pltpu.VMEM((4, 4, SEL, 768), BF16),
            pltpu.VMEM((4, 2, 2, 2, SEL, OC), BF16),
            pltpu.VMEM((4, 2, 2, SEL, OC), BF16),
            pltpu.VMEM((4, 2, 2, SEL, OC), BF16),
            pltpu.VMEM((4, 2, SEL, OC), BF16),
            pltpu.VMEM((4, 2, SEL, OC), BF16),
            pltpu.VMEM((4, 2, SEL, OC), BF16),
            pltpu.SemaphoreType.DMA((SEMS,)),
            pltpu.SemaphoreType.DMA((SEMS,)),
            pltpu.SemaphoreType.DMA((4 + NP,)),
        ],
        compiler_params=pltpu.CompilerParams(
            collective_id=0, has_side_effects=True, vmem_limit_bytes=52 * 2**20),
    )(owners, positions, sel_rows, norm_gain, jnp.asarray(FREQ),
      sel_hidden, w_query, w_keyval, store, w_out)
    return blended[None], mixed[None]


def solution(mesh):
    return jax.shard_map(
        shards,
        mesh=mesh,
        in_specs=(
            P("section", None, "tensor"),
            P(),
            P(),
            P(),
            P(None, None, "section"),
            P("section"),
            P("section", "tensor"),
            P("section", "tensor"),
            P("tensor", "section"),
        ),
        out_specs=(P("section", None, "tensor"), P("tensor", None, "section")),
        check_vma=False,
    )
```

time: 161 us -> 145 us (0.901)
  the two profiles are of different devices: /device:TPU:90 before, /device:TPU:36 now
where the time goes in v3:
time: 145 us
  Pallas kernels  138 us (95%)
  local copies, waits for them, and re-layouts  6.68 us (5%)
    pallas_call x1, Pallas kernels, shards(): pl.pallas_call(sublayer, name='sublayer', out_shape=(jax.ShapeDtypeStruct...  138 us
    unnamed x16, local copies, waits for them, and re-layouts  6.68 us

profile of v3, /device:TPU:36, one launch (start us, length us, event | category | flops | bytes accessed | tf_op | source)
XLA Modules:
  0.0 145.0 jit_solution(15483562939602078281)
XLA Ops:
  0.6 0.0 copy-start
  0.6 1.1 copy-done
  1.7 0.0 copy-start.1
  1.7 0.9 copy-done.1
  2.6 0.0 copy-start.2
  2.7 0.7 copy-done.2
  3.3 0.0 copy-start.3
  3.3 0.7 copy-done.3
  4.0 0.0 copy-start.4
  4.0 0.7 copy-done.4
  4.7 0.0 copy-start.5
  4.7 0.7 copy-done.5
  5.3 0.0 copy-start.6
  5.3 0.7 copy-done.6
  6.0 137.7 %sublayer.1 = (bf16[640,128]{1,0:T(8,128)(2,1)S(1)}, bf16[96,768]{1,0:T(8,128)(2,1)S(1)}) custom-call(s32[16]{0:T(128)S(1)} %copy-done.4, s32[16]{0:T(128)S(1)} %copy-done.5, s32[16,96]{1,0:T(8,128)S(1)} %copy-done.2, bf16[768]{0:T(1024)(128)(2,1)S(1)} %copy-done.3, f32[1,128]{1,0:T(1,128)S(1)} %copy-done.6, bf16[16,96,768]{2,1,0:T(8,128)(2,1)} %h_any.1, ...), custom_call_target="tpu_custom_call" | custom-call | tf_op jit(solution)/shard_map/sublayer/pallas_call | solution.py:508
  143.7 0.7 copy.14
  144.3 0.7 copy.15
Async XLA Ops:
  0.6 1.1 copy-start
  1.7 0.9 copy-start.1
  2.6 0.7 copy-start.2
  3.3 0.7 copy-start.3
  4.0 0.7 copy-start.4
  4.7 0.7 copy-start.5
  5.3 0.7 copy-start.6

commit v4 on v3

--- a/solution.py
+++ b/solution.py
@@ -23,13 +23,20 @@
 QN = HALF * SEL
 QC = 2 * SEL
 TQ = 4 * QC
-PARTS = [(0, 128), (128, 256), (384, 256)]
+PARTS = [(0, 192), (192, 256), (448, 192)]
 NP = len(PARTS)
 OC = 384
 SCALE2 = math.log2(math.e) / math.sqrt(HD)
 CHUNKS = [(0, 128), (128, 256), (384, 256), (640, 256)]
-XBASE = 180
-SEMS = 200
+XBASE = 190
+ORDER = (
+    "s0", "a0", "s1", "m2", "f0", "f1", "s2", "r0", "m3", "m0", "F0", "r1", "F1", "m1",
+    "f2", "t0", "r2", "N1", "t1", "N0", "o0", "t2", "F2", "Z0", "o1", "F3", "N2", "q0",
+    "Z1", "o2", "E0", "p2", "p0", "N3", "Z2", "p1", "G0", "Q0", "Z3", "P0", "Q1", "A0",
+    "Q2", "A1", "M0", "A2", "M1", "H0", "M2", "H1", "I1", "I0", "I2", "H2", "K1", "K0",
+    "R0", "K2",
+)
+SEMS = 210
 
 
 def spread(vec, lanes):
@@ -46,8 +53,8 @@
 def sublayer(owners, positions, rows, gain, freq, h_any, wq_any, wkv_any, store, wo_any,
              blended, mixed,
              h, wq, wkv, wo, st0, st1, st2, stsend, strecv, p2, p2r, acc, psend, precv, zsend,
-             zrecv, sqs, sqr, sqz, sqzr, trig, kvc, fr, keys, vt, first_kv, q, sbuf, pbuf, o, lse,
-             orecv, lrecv, ag, prod, crecv, csum, zlrecv, xsum, xrecv, ssem, rsem, lsem):
+             zrecv, sqs, sqr, sqz, sqzr, scale, trig, kvc, fr, keys, vt, first_kv, q, sbuf, pbuf, o, lse,
+             orecv, lrecv, ag, prod, crecv, csum, zlrecv, xsum, xrecv, xwide, fin, ssem, rsem, lsem):
     s = lax.axis_index("section")
     t = lax.axis_index("tensor")
     y, z = s // 4, s % 4
@@ -152,23 +159,23 @@
                 precision=lax.Precision.HIGHEST, preferred_element_type=F32)
             sqs[d, g:g + 1, :SEL] = row[:1]
 
-    up2, dn2, up1, dn1 = [], [], [], []
+    up2, dn2, up1, dn1 = {}, {}, {}, {}
 
     def send_far(k):
         cols = pl.ds(*CHUNKS[k])
-        up2.append(push(p2.at[0, pl.ds(0, 2), :, cols], p2r.at[0, :, :, cols], ypeer(1)))
-        dn2.append(push(p2.at[0, pl.ds(2, 2), :, cols], p2r.at[1, :, :, cols], ypeer(3)))
+        up2[k] = push(p2.at[0, pl.ds(0, 2), :, cols], p2r.at[0, :, :, cols], ypeer(1))
+        dn2[k] = push(p2.at[0, pl.ds(2, 2), :, cols], p2r.at[1, :, :, cols], ypeer(3))
 
     def send_near(k):
         cols = pl.ds(*CHUNKS[k])
         up2[k].wait_recv()
         psend[0, :2, :, cols] = (acc[1, :2, :, cols] + p2r[0, :, :, cols].astype(F32)).astype(BF16)
         psend[0, 2:, :, cols] = acc[1, 2:, :, cols].astype(BF16)
-        up1.append(push(psend.at[0, :, :, cols], precv.at[0, :, :, cols], ypeer(1)))
+        up1[k] = push(psend.at[0, :, :, cols], precv.at[0, :, :, cols], ypeer(1))
         dn2[k].wait_recv()
         psend[1, 2:, :, cols] = (acc[2, 2:, :, cols] + p2r[1, :, :, cols].astype(F32)).astype(BF16)
         psend[1, :2, :, cols] = acc[2, :2, :, cols].astype(BF16)
-        dn1.append(push(psend.at[1, :, :, cols], precv.at[1, :, :, cols], ypeer(3)))
+        dn1[k] = push(psend.at[1, :, :, cols], precv.at[1, :, :, cols], ypeer(3))
 
     total = acc.at[0]
 
@@ -211,60 +218,57 @@
         kz[7].wait_recv()
         kx.append(push(kvc.at[kind, 2, part], kvc.at[kind, 2, part], partner))
 
-    sa = send_store(0)
-    for c in local[:3]:
-        c.wait()
-    multiply(2, p2, 0)
-    sb = send_store(1)
-    sq_y = [push(sqs.at[2], sqr.at[2], ypeer(2))]
-    fa = forward_store(0, sa)
-    send_far(0)
-    send_far(1)
-    multiply(1, acc, 1)
-    sq_y.append(push(sqs.at[1], sqr.at[3], ypeer(1)))
-    ra = route_store(0, fa)
-    multiply(3, acc, 2)
-    sq_y.append(push(sqs.at[3], sqr.at[1], ypeer(3)))
-    sc = send_store(2)
-    fb = forward_store(1, sb)
-
     row8 = lax.broadcasted_iota(jnp.int32, (8, SEL), 0) == 0
     start = positions[s].astype(F32)
     my_rows = rows[pl.ds(s, 1), :].astype(F32)
-    angle = spread(jnp.where(row8, my_rows + start, 0.0), HD) * freq[...]
-    lane_sign = jnp.where(lax.broadcasted_iota(jnp.int32, (1, HD), 1) < 64, -1.0, 1.0)
-    trig[0, :SEL] = jnp.cos(angle)
-    trig[1, :SEL] = jnp.sin(angle) * lane_sign
-    shift = jnp.broadcast_to(freq[...] * start, (8, HD))
-    trig[0, SEL:] = jnp.where(values, 1.0, jnp.cos(shift))
-    trig[1, SEL:] = jnp.where(values, 0.0, jnp.sin(shift) * lane_sign)
-    kz_a, kx_a = settle(0, ra)
-    multiply(0, acc, 0)
-    send_far(2)
-    send_far(3)
-    send_near(0)
-    send_near(1)
-    waits(sq_y)
-    sqz[...] = sqs[0] + sqr[1] + sqr[2] + sqr[3]
-    sq_z = [push(sqz, sqzr.at[4 - d], zpeer(d)) for d in (1, 3, 2)]
-    rb = route_store(1, fb)
-    pass_on(0, kz_a, kx_a)
-    fc = forward_store(2, sc)
-    kz_b, kx_b = settle(1, rb)
-    send_near(2)
-    pass_far(0, kz_a, kx_a)
-    pz = [send_z(0)]
-    rc = route_store(2, fc)
-    send_near(3)
-    pass_on(1, kz_b, kx_b)
-    pz.append(send_z(1))
-    kz_c, kx_c = settle(2, rc)
-    pass_far(1, kz_b, kx_b)
-
-    waits(sq_z)
-    squares = sqz[...] + sqzr[1] + sqzr[2] + sqzr[3]
-    own = lax.broadcasted_iota(jnp.int32, (8, 128), 0) == z
-    inv = lax.rsqrt(spread(jnp.where(own, squares, 0.0), HD)[:SEL] / D + EPS)
+
+    def angles():
+        angle = spread(jnp.where(row8, my_rows + start, 0.0), HD) * freq[...]
+        lane_sign = jnp.where(lax.broadcasted_iota(jnp.int32, (1, HD), 1) < 64, -1.0, 1.0)
+        trig[0, :SEL] = jnp.cos(angle)
+        trig[1, :SEL] = jnp.sin(angle) * lane_sign
+        shift = jnp.broadcast_to(freq[...] * start, (8, HD))
+        trig[0, SEL:] = jnp.where(values, 1.0, jnp.cos(shift))
+        trig[1, SEL:] = jnp.where(values, 0.0, jnp.sin(shift) * lane_sign)
+
+    sends, fars, routes, kz, kx, pz, qy = {}, {}, {}, {}, {}, {}, {}
+    sq_y, sq_z, fz, fx = [], [], {}, []
+
+    def do_send(k):
+        sends[k] = send_store(k)
+
+    def do_forward(k):
+        fars[k] = forward_store(k, sends[k])
+
+    def do_route(k):
+        routes[k] = route_store(k, fars[k])
+
+    def do_settle(k):
+        kz[k], kx[k] = settle(k, routes[k])
+
+    def do_multiply(d):
+        if d == 2:
+            for c in local[:3]:
+                c.wait()
+            multiply(2, p2, 0)
+        else:
+            multiply(d, acc, {1: 1, 3: 2, 0: 0}[d])
+        if d:
+            sq_y.append(push(sqs.at[d], sqr.at[4 - d], ypeer(d)))
+
+    def do_z(k):
+        pz[k] = send_z(k)
+
+    def do_squares(_):
+        waits(sq_y)
+        sqz[...] = sqs[0] + sqr[1] + sqr[2] + sqr[3]
+        sq_z.extend(push(sqz, sqzr.at[4 - d], zpeer(d)) for d in (1, 3, 2))
+
+    def factor():
+        waits(sq_z)
+        squares = sqz[...] + sqzr[1] + sqzr[2] + sqzr[3]
+        own = lax.broadcasted_iota(jnp.int32, (8, 128), 0) == z
+        return lax.rsqrt(spread(jnp.where(own, squares, 0.0), HD)[:SEL] / D + EPS)
 
     def summed(lo):
         cols = pl.ds(lo, HD)
@@ -272,17 +276,22 @@
              + precv[1, z, :, cols].astype(F32))
         for d in (1, 2, 3):
             v = v + zrecv[d, :, cols].astype(F32)
-        return v * inv
-
-    waits(pz[0])
-    fr[kind, 0] = turned(
-        summed(0), jnp.where(values, 1.0, trig[0, :SEL]),
-        jnp.where(values, 0.0, trig[1, :SEL])).astype(BF16)
-    fz = {4 - d: push(fr.at[kind, 0], fr.at[kind, 4 - d], zpeer(d)) for d in (1, 3, 2)}
-    fx = [push(fr.at[kind, 0], fr.at[kind, 0], partner)]
-    pass_on(2, kz_c, kx_c)
-    pz.append(send_z(2))
-    qy = []
+        return v * scale[...]
+
+    def do_fresh(_):
+        scale[...] = factor()
+        waits(pz[0])
+        fr[kind, 0] = turned(
+            summed(0), jnp.where(values, 1.0, trig[0, :SEL]),
+            jnp.where(values, 0.0, trig[1, :SEL])).astype(BF16)
+        for d in (1, 3, 2):
+            fz[4 - d] = push(fr.at[kind, 0], fr.at[kind, 4 - d], zpeer(d))
+        fx.append(push(fr.at[kind, 0], fr.at[kind, 0], partner))
+
+    def do_fresh_over(_):
+        for r in (3, 1, 2):
+            fz[r].wait_recv()
+            fx.append(push(fr.at[kind, r], fr.at[kind, r], partner))
 
     def send_queries(k):
         waits(pz[k + 1])
@@ -290,36 +299,28 @@
             q[k, j * SEL:(j + 1) * SEL] = turned(
                 summed(HD + (2 * k + j) * HD), trig[0, :SEL], trig[1, :SEL]).astype(BF16)
         mine = q.at[k, pl.ds(0, QC)]
-        qy.append([push(mine, q.at[k, pl.ds((4 - d) * QC, QC)], ypeer(d)) for d in (1, 3, 2)])
-
-    send_queries(0)
-    pass_far(2, kz_c, kx_c)
-    for r in (3, 1, 2):
-        fz[r].wait_recv()
-        fx.append(push(fr.at[kind, r], fr.at[kind, r], partner))
-    pz.append(send_z(3))
-    send_queries(1)
-
-    waits(kx_a)
-    waits(kx_b)
-    waits(kx_c)
-    waits(fx)
-    for r in range(4):
-        group = rows[pl.ds(y * 4 + (z + r) % 4, 1), :]
-        hit = lax.broadcasted_iota(jnp.int32, (L, SEL), 0) == group
-        hot = jnp.where(hit, 1.0, 0.0)
-        taken = jnp.max(hot, axis=1, keepdims=True) > 0.0
-        hot = hot.astype(BF16)
-        for k in (0, 1):
-            placed = jnp.dot(hot, fr[k, r], preferred_element_type=F32)
-            patched = jnp.where(taken, placed, kvc[k, r].astype(F32))
-            if r == 0:
-                first_kv[k] = patched.astype(BF16)
-            if k == 0:
-                keys[r] = patched.astype(BF16)
-            else:
-                vt[:, r * L:(r + 1) * L] = patched.T.astype(BF16)
-    blended[...] = first_kv[kind]
+        qy[k] = [push(mine, q.at[k, pl.ds((4 - d) * QC, QC)], ypeer(d)) for d in (1, 3, 2)]
+
+    def do_patch(_):
+        for copies in kx.values():
+            waits(copies)
+        waits(fx)
+        for r in range(4):
+            group = rows[pl.ds(y * 4 + (z + r) % 4, 1), :]
+            hit = lax.broadcasted_iota(jnp.int32, (L, SEL), 0) == group
+            hot = jnp.where(hit, 1.0, 0.0)
+            taken = jnp.max(hot, axis=1, keepdims=True) > 0.0
+            hot = hot.astype(BF16)
+            for k in (0, 1):
+                placed = jnp.dot(hot, fr[k, r], preferred_element_type=F32)
+                patched = jnp.where(taken, placed, kvc[k, r].astype(F32))
+                if r == 0:
+                    first_kv[k] = patched.astype(BF16)
+                if k == 0:
+                    keys[r] = patched.astype(BF16)
+                else:
+                    vt[:, r * L:(r + 1) * L] = patched.T.astype(BF16)
+        blended[...] = first_kv[kind]
 
     lane = lax.broadcasted_iota(jnp.int32, (1, TQ), 1)
     first = jnp.full((1, TQ), positions[y * 4 + z], jnp.int32)
@@ -401,8 +402,8 @@
         send_y(k, 0)
         zs[k, 2] = push(mine, mine, zpeer(2))
 
-    def gather_z(k):
-        for d in (3, 1, 2):
+    def gather_z(k, blocks):
+        for d in blocks:
             zs[k, 4 - d].wait_recv()
             send_y(k, d)
 
@@ -428,9 +429,12 @@
         csum[r, c] = (prod[r, c, core].astype(F32) + crecv[r, c].astype(F32)).astype(BF16)
         return push(csum.at[r, c, 1 - zl], zlrecv.at[r, c], pair)
 
+    wide = (1, 3)
+
     def x_copy(r, c, slot):
+        src, dst = (csum, xwide) if r in wide else (xsum, xrecv)
         return pltpu.make_async_remote_copy(
-            src_ref=xsum.at[r, c], dst_ref=xrecv.at[slot, c], send_sem=ssem.at[XBASE + 2 * r + c],
+            src_ref=src.at[r, c], dst_ref=dst.at[slot, c], send_sem=ssem.at[XBASE + 2 * r + c],
             recv_sem=rsem.at[XBASE + 2 * slot + c], device_id=xpeer(4 - slot),
             device_id_type=MESH)
 
@@ -439,55 +443,91 @@
 
     def send_x(r, c, copy):
         copy.wait_recv()
-        xsum[r, c] = (csum[r, c, zl].astype(F32) + zlrecv[r, c].astype(F32)).astype(BF16)
+        if r in wide:
+            csum[r, c] = (prod[r, c, core].astype(F32) + crecv[r, c].astype(F32)).astype(BF16)
+        else:
+            xsum[r, c] = (csum[r, c, zl].astype(F32) + zlrecv[r, c].astype(F32)).astype(BF16)
 
         @pl.when(away(r) != 0)
         def _():
             x_copy(r, c, (4 - away(r)) % 4).start()
 
-    g0 = attend(0)
-    send_queries(2)
-    g1 = attend(1)
-    gather_start(0, g0)
-    g2 = attend(2)
-    gather_z(0)
-    gather_start(1, g1)
-    gather_z(1)
-    gather_start(2, g2)
-    gather_far(0)
-    gather_z(2)
-    gather_far(1)
-    local[3 + NP].wait()
-    tw = {(0, c): multiply_out(0, c) for c in (0, 1)}
-    gather_far(2)
-    zz = {}
-    for r in (1, 3):
+    parts, tw = {}, {}
+
+    def do_product(r):
+        if not tw:
+            local[3 + NP].wait()
         for c in (0, 1):
             tw[r, c] = multiply_out(r, c)
-    for r in (0, 1, 3):
+
+    def do_attend(k):
+        parts[k] = attend(k)
+
+    steps = {
+        "s": do_send, "f": do_forward, "r": do_route, "t": do_settle,
+        "o": lambda k: pass_on(k, kz[k], kx[k]), "p": lambda k: pass_far(k, kz[k], kx[k]),
+        "m": do_multiply, "F": send_far, "N": send_near, "Z": do_z, "a": lambda _: angles(),
+        "q": do_squares, "E": do_fresh, "G": do_fresh_over, "Q": send_queries, "P": do_patch,
+        "A": do_attend, "M": lambda k: gather_start(k, parts[k]),
+        "H": lambda k: gather_z(k, (3, 1)), "I": lambda k: gather_z(k, (2,)), "K": gather_far,
+        "R": do_product,
+    }
+    for step in ORDER:
+        steps[step[0]](int(step[1]))
+    zz = {}
+    for c in (0, 1):
+        zz[0, c] = send_zl(0, c, tw[0, c])
+    do_product(1)
+    do_product(3)
+    for r in wide:
         for c in (0, 1):
-            zz[r, c] = send_zl(r, c, tw[r, c])
+            send_x(r, c, tw[r, c])
     for c in (0, 1):
         send_x(0, c, zz[0, c])
     for k in range(3):
         for d in (0, 3, 1, 2):
             fw[k, d].wait_recv()
-    for c in (0, 1):
-        tw[2, c] = multiply_out(2, c)
-    for r in (1, 3):
-        for c in (0, 1):
-            send_x(r, c, zz[r, c])
+    do_product(2)
     for c in (0, 1):
         zz[2, c] = send_zl(2, c, tw[2, c])
     for c in (0, 1):
         send_x(2, c, zz[2, c])
     home = (x + 4 - y) % 4
-    for c in (0, 1):
-        v = xsum[home, c].astype(F32)
-        for slot in (1, 2, 3):
-            x_copy(0, c, slot).wait_recv()
-            v = v + xrecv[slot, c].astype(F32)
-        mixed[:, c * OC:(c + 1) * OC] = v.astype(BF16)
+
+    @pl.when(home % 2 == 0)
+    def _():
+        for c in (0, 1):
+            v = xsum[home, c].astype(F32)
+            for slot in (1, 2, 3):
+                x_copy(0, c, slot).wait_recv()
+                v = v + xrecv[slot, c].astype(F32)
+            mixed[:, c * OC:(c + 1) * OC] = v.astype(BF16)
+
+    @pl.when(home % 2 == 1)
+    def _():
+        last = []
+        for c in (0, 1):
+            for slot in (1, 2, 3):
+                x_copy(1, c, slot).wait_recv()
+            both = []
+            for k in (1 - zl, zl):
+                v = csum[home, c, k].astype(F32)
+                for slot in (1, 2, 3):
+                    v = v + xwide[slot, c, k].astype(F32)
+                both.append(v)
+            xsum[1, c] = both[0].astype(BF16)
+            copy = pltpu.make_async_remote_copy(
+                src_ref=xsum.at[1, c], dst_ref=zlrecv.at[1, c], send_sem=ssem.at[XBASE + 8 + c],
+                recv_sem=rsem.at[XBASE + 8 + c], device_id=pair, device_id_type=MESH)
+            copy.start()
+            last.append(copy)
+            fin[c] = both[1]
+        for c in (0, 1):
+            last[c].wait_recv()
+            mixed[:, c * OC:(c + 1) * OC] = (fin[c] + zlrecv[1, c].astype(F32)).astype(BF16)
+        for c in (0, 1):
+            last[c].wait_send()
+
     for r in range(4):
         @pl.when(away(r) != 0)
         def _():
@@ -500,7 +540,7 @@
 
 VM = pl.BlockSpec(memory_space=pltpu.VMEM)
 SM = pl.BlockSpec(memory_space=pltpu.SMEM)
-ANY = pl.BlockSpec(memory_space=pl.ANY)
+HBM = pl.BlockSpec(memory_space=pltpu.HBM)
 FREQ = (THETA ** (-2.0 * (np.arange(HD) % (HD // 2)) / HD)).astype(np.float32)[None]
 
 
@@ -512,7 +552,7 @@
             jax.ShapeDtypeStruct((L, HD), BF16),
             jax.ShapeDtypeStruct((SEL, 768), BF16),
         ),
-        in_specs=[SM, SM, VM, VM, VM, ANY, ANY, ANY, ANY, ANY],
+        in_specs=[SM, SM, VM, VM, VM, HBM, HBM, HBM, HBM, HBM],
         out_specs=(VM, VM),
         scratch_shapes=[
             pltpu.VMEM((16, SEL, 768), BF16),
@@ -533,6 +573,7 @@
             pltpu.VMEM((4, 8, 128), F32),
             pltpu.VMEM((8, 128), F32),
             pltpu.VMEM((4, 8, 128), F32),
+            pltpu.VMEM((SEL, HD), F32),
             pltpu.VMEM((2, SEL + 8, HD), F32),
             pltpu.VMEM((2, 4, L, HD), BF16),
             pltpu.VMEM((2, 4, SEL, HD), BF16),
@@ -553,12 +594,14 @@
             pltpu.VMEM((4, 2, SEL, OC), BF16),
             pltpu.VMEM((4, 2, SEL, OC), BF16),
             pltpu.VMEM((4, 2, SEL, OC), BF16),
+            pltpu.VMEM((4, 2, 2, SEL, OC), BF16),
+            pltpu.VMEM((2, SEL, OC), F32),
             pltpu.SemaphoreType.DMA((SEMS,)),
             pltpu.SemaphoreType.DMA((SEMS,)),
             pltpu.SemaphoreType.DMA((4 + NP,)),
         ],
         compiler_params=pltpu.CompilerParams(
-            collective_id=0, has_side_effects=True, vmem_limit_bytes=52 * 2**20),
+            collective_id=0, has_side_effects=True, vmem_limit_bytes=60 * 2**20),
     )(owners, positions, sel_rows, norm_gain, jnp.asarray(FREQ),
       sel_hidden, w_query, w_keyval, store, w_out)
     return blended[None], mixed[None]

time: 145 us -> 130 us (0.90)
  the two profiles are of different devices: /device:TPU:36 before, /device:TPU:8 now
where the time goes in v4:
time: 130 us
  Pallas kernels  126 us (97%)
  local copies, waits for them, and re-layouts  3.17 us (2%)
    pallas_call x1, Pallas kernels, shards(): pl.pallas_call(sublayer, name='sublayer', out_shape=(jax.ShapeDtypeStruct...  126 us
    unnamed x2, local copies, waits for them, and re-layouts  3.17 us

profile of v4, /device:TPU:8, one launch (start us, length us, event | category | flops | bytes accessed | tf_op | source)
XLA Modules:
  0.0 129.7 jit_solution(17998489915928219794)
XLA Ops:
  0.6 125.9 %sublayer.1 = (bf16[640,128]{1,0:T(8,128)(2,1)}, bf16[96,768]{1,0:T(8,128)(2,1)}) custom-call(s32[16]{0:T(128)} %owners.1, s32[16]{0:T(128)} %positions.1, s32[16,96]{1,0:T(8,128)} %rows.1, bf16[768]{0:T(1024)(128)(2,1)} %gain.1, f32[1,128]{1,0:T(1,128)} %constant.2.clone.freq, bf16[16,96,768]{2,1,0:T(8,128)(2,1)} %h_any.1, bf16[768,768]{1,0:T(8,128)(2,1)} %wq_any.1, ...), custom_call_target="tpu_custom_call" | custom-call | tf_op jit(solution)/shard_map/sublayer/pallas_call | solution.py:548
  126.6 1.6 %copy.14 = bf16[1,640,128]{2,1,0:T(8,128)(2,1)} copy(bf16[1,640,128]{2,1,0:T(8,128)(2,1)} %bitcast.2) | data formatting | bytes 327680
  128.2 1.6 %copy.15 = bf16[1,96,768]{2,1,0:T(8,128)(2,1)} copy(bf16[1,96,768]{2,1,0:T(8,128)(2,1)} %bitcast.3) | data formatting | bytes 294912

commit v5 on v4

--- a/solution.py
+++ b/solution.py
@@ -25,16 +25,17 @@
 TQ = 4 * QC
 PARTS = [(0, 192), (192, 256), (448, 192)]
 NP = len(PARTS)
-OC = 384
 SCALE2 = math.log2(math.e) / math.sqrt(HD)
-CHUNKS = [(0, 128), (128, 256), (384, 256), (640, 256)]
+RC = SEL // 3
 XBASE = 190
 ORDER = (
-    "s0", "a0", "s1", "m2", "f0", "f1", "s2", "r0", "m3", "m0", "F0", "r1", "F1", "m1",
-    "f2", "t0", "r2", "N1", "t1", "N0", "o0", "t2", "F2", "Z0", "o1", "F3", "N2", "q0",
-    "Z1", "o2", "E0", "p2", "p0", "N3", "Z2", "p1", "G0", "Q0", "Z3", "P0", "Q1", "A0",
-    "Q2", "A1", "M0", "A2", "M1", "H0", "M2", "H1", "I1", "I0", "I2", "H2", "K1", "K0",
-    "R0", "K2",
+    "s0", "a0", "s1", "m2", "f0", "m1", "f1", "r0", "s2", "r1", "m3", "f2", "m0", "F0",
+    "t0", "F1", "q0", "F2", "r2", "t1", "N0", "N1", "o0", "Z0", "o1", "t2", "F3", "Z1",
+    "E0", "N2", "p0", "o2", "p1", "N3", "Z2", "G0", "p2", "Q0", "Z3", "P0", "Q1", "A0",
+    "Q2", "A1", "M0", "A2", "M1", "H0", "I0", "M2", "R00", "H1", "X00", "I1", "R01", "K0",
+    "R30", "X01", "X30", "R10", "I2", "H2", "R02", "X10", "K1", "R31", "X02", "R11", "R20", "X31",
+    "X20", "X11", "K2", "R12", "R21", "R32", "X12", "X21", "R22", "X32", "X22", "D1", "D0", "D2",
+    "C0", "C1", "C2",
 )
 SEMS = 210
 
@@ -54,7 +55,7 @@
              blended, mixed,
              h, wq, wkv, wo, st0, st1, st2, stsend, strecv, p2, p2r, acc, psend, precv, zsend,
              zrecv, sqs, sqr, sqz, sqzr, scale, trig, kvc, fr, keys, vt, first_kv, q, sbuf, pbuf, o, lse,
-             orecv, lrecv, ag, prod, crecv, csum, zlrecv, xsum, xrecv, xwide, fin, ssem, rsem, lsem):
+             orecv, lrecv, ag, prod, crecv, csum, xrecv, zlsend, zlrecv, fin, ssem, rsem, lsem):
     s = lax.axis_index("section")
     t = lax.axis_index("tensor")
     y, z = s // 4, s % 4
@@ -161,34 +162,39 @@
 
     up2, dn2, up1, dn1 = {}, {}, {}, {}
 
+    def chunk(k):
+        if k == 0:
+            return pl.ds(0, SEL), pl.ds(0, HD)
+        return pl.ds((k - 1) * RC, RC), pl.ds(HD, 768)
+
     def send_far(k):
-        cols = pl.ds(*CHUNKS[k])
-        up2[k] = push(p2.at[0, pl.ds(0, 2), :, cols], p2r.at[0, :, :, cols], ypeer(1))
-        dn2[k] = push(p2.at[0, pl.ds(2, 2), :, cols], p2r.at[1, :, :, cols], ypeer(3))
+        at = chunk(k)
+        up2[k] = push(p2.at[0, pl.ds(0, 2), *at], p2r.at[0, :, *at], ypeer(1))
+        dn2[k] = push(p2.at[0, pl.ds(2, 2), *at], p2r.at[1, :, *at], ypeer(3))
 
     def send_near(k):
-        cols = pl.ds(*CHUNKS[k])
+        at = chunk(k)
         up2[k].wait_recv()
-        psend[0, :2, :, cols] = (acc[1, :2, :, cols] + p2r[0, :, :, cols].astype(F32)).astype(BF16)
-        psend[0, 2:, :, cols] = acc[1, 2:, :, cols].astype(BF16)
-        up1[k] = push(psend.at[0, :, :, cols], precv.at[0, :, :, cols], ypeer(1))
+        psend[0, :2, *at] = (acc[1, :2, *at] + p2r[0, :, *at].astype(F32)).astype(BF16)
+        psend[0, 2:, *at] = acc[1, 2:, *at].astype(BF16)
+        up1[k] = push(psend.at[0, :, *at], precv.at[0, :, *at], ypeer(1))
         dn2[k].wait_recv()
-        psend[1, 2:, :, cols] = (acc[2, 2:, :, cols] + p2r[1, :, :, cols].astype(F32)).astype(BF16)
-        psend[1, :2, :, cols] = acc[2, :2, :, cols].astype(BF16)
-        dn1[k] = push(psend.at[1, :, :, cols], precv.at[1, :, :, cols], ypeer(3))
+        psend[1, 2:, *at] = (acc[2, 2:, *at] + p2r[1, :, *at].astype(F32)).astype(BF16)
+        psend[1, :2, *at] = acc[2, :2, *at].astype(BF16)
+        dn1[k] = push(psend.at[1, :, *at], precv.at[1, :, *at], ypeer(3))
 
     total = acc.at[0]
 
     def send_z(k):
-        cols = pl.ds(*CHUNKS[k])
+        at = chunk(k)
         up1[k].wait_recv()
         dn1[k].wait_recv()
         out = []
         for d in (1, 3, 2):
             g = (z + d) % 4
-            zsend[d, :, cols] = (total[g, :, cols] + precv[0, g, :, cols].astype(F32)
-                                 + precv[1, g, :, cols].astype(F32)).astype(BF16)
-            out.append(push(zsend.at[d, :, cols], zrecv.at[4 - d, :, cols], zpeer(d)))
+            zsend[d, *at] = (total[g, *at] + precv[0, g, *at].astype(F32)
+                             + precv[1, g, *at].astype(F32)).astype(BF16)
+            out.append(push(zsend.at[d, *at], zrecv.at[4 - d, *at], zpeer(d)))
         return out
 
     def settle(k, copies):
@@ -270,19 +276,17 @@
         own = lax.broadcasted_iota(jnp.int32, (8, 128), 0) == z
         return lax.rsqrt(spread(jnp.where(own, squares, 0.0), HD)[:SEL] / D + EPS)
 
-    def summed(lo):
-        cols = pl.ds(lo, HD)
-        v = (total[z, :, cols] + precv[0, z, :, cols].astype(F32)
-             + precv[1, z, :, cols].astype(F32))
+    def summed(at):
+        v = total[z, *at] + precv[0, z, *at].astype(F32) + precv[1, z, *at].astype(F32)
         for d in (1, 2, 3):
-            v = v + zrecv[d, :, cols].astype(F32)
-        return v * scale[...]
+            v = v + zrecv[d, *at].astype(F32)
+        return v * scale[at[0]]
 
     def do_fresh(_):
         scale[...] = factor()
         waits(pz[0])
         fr[kind, 0] = turned(
-            summed(0), jnp.where(values, 1.0, trig[0, :SEL]),
+            summed(chunk(0)), jnp.where(values, 1.0, trig[0, :SEL]),
             jnp.where(values, 0.0, trig[1, :SEL])).astype(BF16)
         for d in (1, 3, 2):
             fz[4 - d] = push(fr.at[kind, 0], fr.at[kind, 4 - d], zpeer(d))
@@ -295,9 +299,11 @@
 
     def send_queries(k):
         waits(pz[k + 1])
-        for j in (0, 1):
-            q[k, j * SEL:(j + 1) * SEL] = turned(
-                summed(HD + (2 * k + j) * HD), trig[0, :SEL], trig[1, :SEL]).astype(BF16)
+        lines = pl.ds(k * RC, RC)
+        for j in range(HALF):
+            q[k, j * RC:(j + 1) * RC] = turned(
+                summed((lines, pl.ds(HD + j * HD, HD))),
+                trig[0, lines], trig[1, lines]).astype(BF16)
         mine = q.at[k, pl.ds(0, QC)]
         qy[k] = [push(mine, q.at[k, pl.ds((4 - d) * QC, QC)], ypeer(d)) for d in (1, 3, 2)]
 
@@ -326,16 +332,20 @@
     first = jnp.full((1, TQ), positions[y * 4 + z], jnp.int32)
     for d in (1, 2, 3):
         first = jnp.where(lane >= d * QC, positions[((y + d) % 4) * 4 + z], first)
-    tiled = (lax.broadcasted_iota(jnp.int32, (SEL, TQ), 1) % SEL
-             == lax.broadcasted_iota(jnp.int32, (SEL, TQ), 0))
-    limit = lax.dot_general(
-        jnp.where(row8, my_rows, 0.0), jnp.where(tiled, 1.0, 0.0), (((1,), (0,)), ((), ())),
-        precision=lax.Precision.HIGHEST, preferred_element_type=F32)[:1]
-    limit = jnp.where(lane < QC, limit, float(L))
+
+    def limits(k):
+        tiled = (lax.broadcasted_iota(jnp.int32, (SEL, TQ), 1) % RC + k * RC
+                 == lax.broadcasted_iota(jnp.int32, (SEL, TQ), 0))
+        limit = lax.dot_general(
+            jnp.where(row8, my_rows, 0.0), jnp.where(tiled, 1.0, 0.0), (((1,), (0,)), ((), ())),
+            precision=lax.Precision.HIGHEST, preferred_element_type=F32)[:1]
+        return jnp.where(lane < QC, limit, float(L))
+
     hidden = [positions[y * 4 + (z + e) % 4] > first for e in range(4)]
 
     def attend(k):
         waits(qy[k])
+        limit = limits(k)
         block = q[k]
         top = jnp.full((1, TQ), MASKED, F32)
         for e in range(4):
@@ -381,14 +391,14 @@
             part = o[k, :QC] if r == 0 else orecv[k, r]
             col = spread(jnp.where(line, share[r] / whole, 0.0), HD)[:QC]
             merged = merged + part.astype(F32) * col
-        for j in (0, 1):
-            lo = (2 * k + j) * HD
-            ag[0, z, :, lo:lo + HD] = merged[j * SEL:(j + 1) * SEL].astype(BF16)
+        for j in range(HALF):
+            ag[0, z, k * RC:(k + 1) * RC, j * HD:(j + 1) * HD] = (
+                merged[j * RC:(j + 1) * RC].astype(BF16))
 
     zs, ups, dns, fw = {}, {}, {}, {}
 
     def block_of(r, k, d):
-        return ag.at[r, (z + d) % 4, :, pl.ds(k * 256, 256)]
+        return ag.at[r, (z + d) % 4, pl.ds(k * RC, RC)]
 
     def send_y(k, d):
         ups[k, d] = push(block_of(0, k, d), block_of(3, k, d), ypeer(1))
@@ -416,49 +426,58 @@
             else:
                 fw[k, d] = push(block_of(1, k, d), block_of(2, k, d), ypeer(3))
 
-    def multiply_out(r, c):
-        cols = pl.ds(c * OC, OC)
-        a = jnp.dot(ag[r].reshape(4 * SEL, 768), wo[:, cols], preferred_element_type=F32)
-        a = a.reshape(4, SEL, OC).astype(BF16)
-        for g in range(4):
-            prod[r, c, g % 2, g // 2] = a[g]
-        return push(prod.at[r, c, 1 - core], crecv.at[r, c], twin)
-
-    def send_zl(r, c, copy):
-        copy.wait_recv()
-        csum[r, c] = (prod[r, c, core].astype(F32) + crecv[r, c].astype(F32)).astype(BF16)
-        return push(csum.at[r, c, 1 - zl], zlrecv.at[r, c], pair)
-
-    wide = (1, 3)
-
-    def x_copy(r, c, slot):
-        src, dst = (csum, xwide) if r in wide else (xsum, xrecv)
+    def x_copy(r, k, slot):
         return pltpu.make_async_remote_copy(
-            src_ref=src.at[r, c], dst_ref=dst.at[slot, c], send_sem=ssem.at[XBASE + 2 * r + c],
-            recv_sem=rsem.at[XBASE + 2 * slot + c], device_id=xpeer(4 - slot),
+            src_ref=csum.at[r, k], dst_ref=xrecv.at[slot, k], send_sem=ssem.at[XBASE + 3 * r + k],
+            recv_sem=rsem.at[XBASE + 3 * slot + k], device_id=xpeer(4 - slot),
             device_id_type=MESH)
 
     def away(r):
         return (y + r + 4 - x) % 4
 
-    def send_x(r, c, copy):
-        copy.wait_recv()
-        if r in wide:
-            csum[r, c] = (prod[r, c, core].astype(F32) + crecv[r, c].astype(F32)).astype(BF16)
-        else:
-            xsum[r, c] = (csum[r, c, zl].astype(F32) + zlrecv[r, c].astype(F32)).astype(BF16)
+    home = (x + 4 - y) % 4
+
+    parts, tw = {}, {}
+
+    def do_product(r, k):
+        if not tw:
+            local[3 + NP].wait()
+        if r == 2:
+            for d in (0, 3, 1, 2):
+                fw[k, d].wait_recv()
+        a = jnp.dot(ag[r, :, k * RC:(k + 1) * RC].reshape(4 * RC, 768), wo[...],
+                    preferred_element_type=F32).reshape(4, RC, 768).astype(BF16)
+        for g in range(4):
+            prod[r, k, g % 2, g // 2] = a[g]
+        tw[r, k] = push(prod.at[r, k, 1 - core], crecv.at[r, k], twin)
+
+    def do_x(r, k):
+        tw[r, k].wait_recv()
+        csum[r, k] = (prod[r, k, core].astype(F32) + crecv[r, k].astype(F32)).astype(BF16)
 
         @pl.when(away(r) != 0)
         def _():
-            x_copy(r, c, (4 - away(r)) % 4).start()
-
-    parts, tw = {}, {}
-
-    def do_product(r):
-        if not tw:
-            local[3 + NP].wait()
-        for c in (0, 1):
-            tw[r, c] = multiply_out(r, c)
+            x_copy(r, k, (4 - away(r)) % 4).start()
+
+    last = {}
+
+    def do_pair(k):
+        for slot in (1, 2, 3):
+            x_copy(0, k, slot).wait_recv()
+
+        def over_x(half):
+            v = csum[home, k, half].astype(F32)
+            for slot in (1, 2, 3):
+                v = v + xrecv[slot, k, half].astype(F32)
+            return v
+
+        zlsend[k] = over_x(1 - zl).astype(BF16)
+        last[k] = push(zlsend.at[k], zlrecv.at[k], pair)
+        fin[k] = over_x(zl)
+
+    def do_close(k):
+        last[k].wait_recv()
+        mixed[k * RC:(k + 1) * RC] = (fin[k] + zlrecv[k].astype(F32)).astype(BF16)
 
     def do_attend(k):
         parts[k] = attend(k)
@@ -470,69 +489,15 @@
         "q": do_squares, "E": do_fresh, "G": do_fresh_over, "Q": send_queries, "P": do_patch,
         "A": do_attend, "M": lambda k: gather_start(k, parts[k]),
         "H": lambda k: gather_z(k, (3, 1)), "I": lambda k: gather_z(k, (2,)), "K": gather_far,
-        "R": do_product,
+        "R": do_product, "X": do_x, "D": do_pair, "C": do_close,
     }
     for step in ORDER:
-        steps[step[0]](int(step[1]))
-    zz = {}
-    for c in (0, 1):
-        zz[0, c] = send_zl(0, c, tw[0, c])
-    do_product(1)
-    do_product(3)
-    for r in wide:
-        for c in (0, 1):
-            send_x(r, c, tw[r, c])
-    for c in (0, 1):
-        send_x(0, c, zz[0, c])
-    for k in range(3):
-        for d in (0, 3, 1, 2):
-            fw[k, d].wait_recv()
-    do_product(2)
-    for c in (0, 1):
-        zz[2, c] = send_zl(2, c, tw[2, c])
-    for c in (0, 1):
-        send_x(2, c, zz[2, c])
-    home = (x + 4 - y) % 4
-
-    @pl.when(home % 2 == 0)
-    def _():
-        for c in (0, 1):
-            v = xsum[home, c].astype(F32)
-            for slot in (1, 2, 3):
-                x_copy(0, c, slot).wait_recv()
-                v = v + xrecv[slot, c].astype(F32)
-            mixed[:, c * OC:(c + 1) * OC] = v.astype(BF16)
-
-    @pl.when(home % 2 == 1)
-    def _():
-        last = []
-        for c in (0, 1):
-            for slot in (1, 2, 3):
-                x_copy(1, c, slot).wait_recv()
-            both = []
-            for k in (1 - zl, zl):
-                v = csum[home, c, k].astype(F32)
-                for slot in (1, 2, 3):
-                    v = v + xwide[slot, c, k].astype(F32)
-                both.append(v)
-            xsum[1, c] = both[0].astype(BF16)
-            copy = pltpu.make_async_remote_copy(
-                src_ref=xsum.at[1, c], dst_ref=zlrecv.at[1, c], send_sem=ssem.at[XBASE + 8 + c],
-                recv_sem=rsem.at[XBASE + 8 + c], device_id=pair, device_id_type=MESH)
-            copy.start()
-            last.append(copy)
-            fin[c] = both[1]
-        for c in (0, 1):
-            last[c].wait_recv()
-            mixed[:, c * OC:(c + 1) * OC] = (fin[c] + zlrecv[1, c].astype(F32)).astype(BF16)
-        for c in (0, 1):
-            last[c].wait_send()
-
+        steps[step[0]](*[int(n) for n in step[1:]])
     for r in range(4):
         @pl.when(away(r) != 0)
         def _():
-            for c in (0, 1):
-                x_copy(r, c, 1).wait_send()
+            for k in range(3):
+                x_copy(r, k, 1).wait_send()
     for c in sent:
         c.wait_send()
     assert ids[0] <= XBASE
@@ -588,14 +553,13 @@
             pltpu.VMEM((3, 4, QC, HD), BF16),
             pltpu.VMEM((3, 4, 8, 256), F32),
             pltpu.VMEM((4, 4, SEL, 768), BF16),
-            pltpu.VMEM((4, 2, 2, 2, SEL, OC), BF16),
-            pltpu.VMEM((4, 2, 2, SEL, OC), BF16),
-            pltpu.VMEM((4, 2, 2, SEL, OC), BF16),
-            pltpu.VMEM((4, 2, SEL, OC), BF16),
-            pltpu.VMEM((4, 2, SEL, OC), BF16),
-            pltpu.VMEM((4, 2, SEL, OC), BF16),
-            pltpu.VMEM((4, 2, 2, SEL, OC), BF16),
-            pltpu.VMEM((2, SEL, OC), F32),
+            pltpu.VMEM((4, 3, 2, 2, RC, 768), BF16),
+            pltpu.VMEM((4, 3, 2, RC, 768), BF16),
+            pltpu.VMEM((4, 3, 2, RC, 768), BF16),
+            pltpu.VMEM((4, 3, 2, RC, 768), BF16),
+            pltpu.VMEM((3, RC, 768), BF16),
+            pltpu.VMEM((3, RC, 768), BF16),
+            pltpu.VMEM((3, RC, 768), F32),
             pltpu.SemaphoreType.DMA((SEMS,)),
             pltpu.SemaphoreType.DMA((SEMS,)),
             pltpu.SemaphoreType.DMA((4 + NP,)),

time: 130 us -> 125 us (0.962)
  the two profiles are of different devices: /device:TPU:8 before, /device:TPU:36 now
where the time goes in v5:
time: 125 us; the launch traced here: 123 us
  Pallas kernels  119 us (95%)
  local copies, waits for them, and re-layouts  3.17 us (3%)
    pallas_call x1, Pallas kernels, shards(): pl.pallas_call(sublayer, name='sublayer', out_shape=(jax.ShapeDtypeStruct...  119 us
    unnamed x2, local copies, waits for them, and re-layouts  3.17 us

profile of v5, /device:TPU:36, one launch (start us, length us, event | category | flops | bytes accessed | tf_op | source)
XLA Modules:
  0.0 122.8 jit_solution(18271177430582049764)
XLA Ops:
  0.6 118.9 %sublayer.1 = (bf16[640,128]{1,0:T(8,128)(2,1)}, bf16[96,768]{1,0:T(8,128)(2,1)}) custom-call(s32[16]{0:T(128)} %owners.1, s32[16]{0:T(128)} %positions.1, s32[16,96]{1,0:T(8,128)} %rows.1, bf16[768]{0:T(1024)(128)(2,1)} %gain.1, f32[1,128]{1,0:T(1,128)} %constant.2.clone.freq, bf16[16,96,768]{2,1,0:T(8,128)(2,1)} %h_any.1, bf16[768,768]{1,0:T(8,128)(2,1)} %wq_any.1, ...), custom_call_target="tpu_custom_call" | custom-call | tf_op jit(solution)/shard_map/sublayer/pallas_call | solution.py:513
  119.6 1.6 %copy.14 = bf16[1,640,128]{2,1,0:T(8,128)(2,1)} copy(bf16[1,640,128]{2,1,0:T(8,128)(2,1)} %bitcast.2) | data formatting | bytes 327680
  121.2 1.6 %copy.15 = bf16[1,96,768]{2,1,0:T(8,128)(2,1)} copy(bf16[1,96,768]{2,1,0:T(8,128)(2,1)} %bitcast.3) | data formatting | bytes 294912

commit v6 on v5

--- a/solution.py
+++ b/solution.py
@@ -29,13 +29,13 @@
 RC = SEL // 3
 XBASE = 190
 ORDER = (
-    "s0", "a0", "s1", "m2", "f0", "m1", "f1", "r0", "s2", "r1", "m3", "f2", "m0", "F0",
-    "t0", "F1", "q0", "F2", "r2", "t1", "N0", "N1", "o0", "Z0", "o1", "t2", "F3", "Z1",
-    "E0", "N2", "p0", "o2", "p1", "N3", "Z2", "G0", "p2", "Q0", "Z3", "P0", "Q1", "A0",
-    "Q2", "A1", "M0", "A2", "M1", "H0", "I0", "M2", "R00", "H1", "X00", "I1", "R01", "K0",
-    "R30", "X01", "X30", "R10", "I2", "H2", "R02", "X10", "K1", "R31", "X02", "R11", "R20", "X31",
-    "X20", "X11", "K2", "R12", "R21", "R32", "X12", "X21", "R22", "X32", "X22", "D1", "D0", "D2",
-    "C0", "C1", "C2",
+    "s0", "a0", "s1", "m2", "f0", "m1", "f1", "r0", "s2", "r1", "m3", "f2", "m0", "B0",
+    "F0", "t0", "F1", "q0", "F2", "r2", "t1", "N0", "N1", "o0", "Z0", "o1", "t2", "F3",
+    "Z1", "E0", "N2", "p0", "o2", "p1", "N3", "Z2", "P0", "G0", "p2", "Q0", "Z3", "P1",
+    "P3", "P2", "Q1", "A0", "Q2", "A1", "M0", "A2", "M1", "H0", "I0", "M2", "R00", "H1",
+    "X00", "I1", "R01", "K0", "R30", "X01", "X30", "R10", "I2", "H2", "R02", "X10", "K1", "R31",
+    "X02", "R11", "R20", "X31", "X20", "X11", "K2", "R12", "R21", "R32", "X12", "X21", "R22", "X32",
+    "X22", "D1", "D0", "D2", "C0", "C1", "C2",
 )
 SEMS = 210
 
@@ -54,7 +54,7 @@
 def sublayer(owners, positions, rows, gain, freq, h_any, wq_any, wkv_any, store, wo_any,
              blended, mixed,
              h, wq, wkv, wo, st0, st1, st2, stsend, strecv, p2, p2r, acc, psend, precv, zsend,
-             zrecv, sqs, sqr, sqz, sqzr, scale, trig, kvc, fr, keys, vt, first_kv, q, sbuf, pbuf, o, lse,
+             zrecv, sqs, sqr, sqz, sqzr, scale, trig, kvc, fr, hots, taken, lim, keys, vt, first_kv, q, sbuf, pbuf, o, lse,
              orecv, lrecv, ag, prod, crecv, csum, xrecv, zlsend, zlrecv, fin, ssem, rsem, lsem):
     s = lax.axis_index("section")
     t = lax.axis_index("tensor")
@@ -307,26 +307,32 @@
         mine = q.at[k, pl.ds(0, QC)]
         qy[k] = [push(mine, q.at[k, pl.ds((4 - d) * QC, QC)], ypeer(d)) for d in (1, 3, 2)]
 
-    def do_patch(_):
+    def do_patch(r):
+        place = {0: 0, 1: 1, 3: 2, 2: 3}[r]
         for copies in kx.values():
-            waits(copies)
-        waits(fx)
+            copies[place].wait_recv()
+        fx[{0: 0, 3: 1, 1: 2, 2: 3}[r]].wait_recv()
+        for k in (0, 1):
+            placed = jnp.dot(hots[r], fr[k, r], preferred_element_type=F32)
+            patched = jnp.where(taken[r] > 0.0, placed, kvc[k, r].astype(F32))
+            if r == 0:
+                first_kv[k] = patched.astype(BF16)
+            if k == 0:
+                keys[r] = patched.astype(BF16)
+            else:
+                vt[:, r * L:(r + 1) * L] = patched.T.astype(BF16)
+        if r == 0:
+            blended[...] = first_kv[kind]
+
+    def do_masks(_):
         for r in range(4):
             group = rows[pl.ds(y * 4 + (z + r) % 4, 1), :]
             hit = lax.broadcasted_iota(jnp.int32, (L, SEL), 0) == group
             hot = jnp.where(hit, 1.0, 0.0)
-            taken = jnp.max(hot, axis=1, keepdims=True) > 0.0
-            hot = hot.astype(BF16)
-            for k in (0, 1):
-                placed = jnp.dot(hot, fr[k, r], preferred_element_type=F32)
-                patched = jnp.where(taken, placed, kvc[k, r].astype(F32))
-                if r == 0:
-                    first_kv[k] = patched.astype(BF16)
-                if k == 0:
-                    keys[r] = patched.astype(BF16)
-                else:
-                    vt[:, r * L:(r + 1) * L] = patched.T.astype(BF16)
-        blended[...] = first_kv[kind]
+            hots[r] = hot.astype(BF16)
+            taken[r] = jnp.broadcast_to(jnp.max(hot, axis=1, keepdims=True), (L, HD))
+        for k in range(3):
+            lim[k] = jnp.broadcast_to(limits(k), (8, TQ))
 
     lane = lax.broadcasted_iota(jnp.int32, (1, TQ), 1)
     first = jnp.full((1, TQ), positions[y * 4 + z], jnp.int32)
@@ -345,7 +351,7 @@
 
     def attend(k):
         waits(qy[k])
-        limit = limits(k)
+        limit = lim[k, :1]
         block = q[k]
         top = jnp.full((1, TQ), MASKED, F32)
         for e in range(4):
@@ -489,7 +495,7 @@
         "q": do_squares, "E": do_fresh, "G": do_fresh_over, "Q": send_queries, "P": do_patch,
         "A": do_attend, "M": lambda k: gather_start(k, parts[k]),
         "H": lambda k: gather_z(k, (3, 1)), "I": lambda k: gather_z(k, (2,)), "K": gather_far,
-        "R": do_product, "X": do_x, "D": do_pair, "C": do_close,
+        "B": do_masks, "R": do_product, "X": do_x, "D": do_pair, "C": do_close,
     }
     for step in ORDER:
         steps[step[0]](*[int(n) for n in step[1:]])
@@ -542,6 +548,9 @@
             pltpu.VMEM((2, SEL + 8, HD), F32),
             pltpu.VMEM((2, 4, L, HD), BF16),
             pltpu.VMEM((2, 4, SEL, HD), BF16),
+            pltpu.VMEM((4, L, SEL), BF16),
+            pltpu.VMEM((4, L, HD), F32),
+            pltpu.VMEM((3, 8, TQ), F32),
             pltpu.VMEM((4, L, HD), BF16),
             pltpu.VMEM((HD, 4 * L), BF16),
             pltpu.VMEM((2, L, HD), BF16),

time: 125 us -> 124 us (level)
  no operation moved by 1% of the time
where the time goes in v6:
time: 124 us; the launch traced here: 123 us
  Pallas kernels  119 us (96%)
  local copies, waits for them, and re-layouts  3.17 us (3%)
    pallas_call x1, Pallas kernels, shards(): pl.pallas_call(sublayer, name='sublayer', out_shape=(jax.ShapeDtypeStruct...  119 us
    unnamed x2, local copies, waits for them, and re-layouts  3.17 us

profile of v6, /device:TPU:36, one launch (start us, length us, event | category | flops | bytes accessed | tf_op | source)
XLA Modules:
  0.0 123.0 jit_solution(15439998307539268653)
XLA Ops:
  0.6 119.2 %sublayer.1 = (bf16[640,128]{1,0:T(8,128)(2,1)}, bf16[96,768]{1,0:T(8,128)(2,1)}) custom-call(s32[16]{0:T(128)} %owners.1, s32[16]{0:T(128)} %positions.1, s32[16,96]{1,0:T(8,128)} %rows.1, bf16[768]{0:T(1024)(128)(2,1)} %gain.1, f32[1,128]{1,0:T(1,128)} %constant.2.clone.freq, bf16[16,96,768]{2,1,0:T(8,128)(2,1)} %h_any.1, bf16[768,768]{1,0:T(8,128)(2,1)} %wq_any.1, ...), custom_call_target="tpu_custom_call" | custom-call | tf_op jit(solution)/shard_map/sublayer/pallas_call | solution.py:519
  119.8 1.6 %copy.14 = bf16[1,640,128]{2,1,0:T(8,128)(2,1)} copy(bf16[1,640,128]{2,1,0:T(8,128)(2,1)} %bitcast.2) | data formatting | bytes 327680
  121.4 1.6 %copy.15 = bf16[1,96,768]{2,1,0:T(8,128)(2,1)} copy(bf16[1,96,768]{2,1,0:T(8,128)(2,1)} %bitcast.3) | data formatting | bytes 294912
